TPU v7x, 32 devices: a whole 2x2x4 slice. The times are simulated.
32 devices in a mesh: grain: 8 (over z, y), cell: 4 (over x, core).
Axes of the slice: x: 2, y: 2, z: 4, core: 2. Of those that a mesh axis runs over, the one named last changes fastest.
Arguments:
- displacement: float32 [1024, 3, 768], P(('grain', 'cell')), may hold values from -0.1 to 0.1
- velocity: float32 [1024, 3, 768], P(('grain', 'cell')), may hold values from -6 to 6
- centers: float32 [3, 1024], P(None, ('grain', 'cell')), may hold values from -4 to 4
- tile_list: int32 [1024, 4, 2], P(('grain', 'cell')), may hold values from 0 to 5
- broken_bits: int32 [1024, 4, 2048], P(('grain', 'cell')), may hold values from 0 to 255, as said below
- surface_nodes: int32 [1024, 512], P(('grain', 'cell')), may hold values from 0 to 767, as said below
- send_order: int32 [32, 128], P(('grain', 'cell')), may hold values from 0 to 127, each once within a row
- pair_list: int32 [32, 128, 2], P(('grain', 'cell')), may hold values from 0 to 127
- pair_count: int32 [32], P(('grain', 'cell')), may hold values from 1 to 128, 2048 in all
Outputs:
- force: float32 [1024, 3, 768], P(('grain', 'cell'))
- new_velocity: float32 [1024, 3, 768], P(('grain', 'cell'))
Inputs may be any that keep to these rules, and one draw needn't show every extreme that they name: `surface_nodes`: within a grain the 512 surface node indices are distinct. `send_order`: each row is a permutation of the device's 128 surface blocks; position p goes to device p div 4, so every device receives exactly 4 blocks from each device. `broken_bits`: each word packs 8 broken flags, any bit pattern.
All inputs are finite; a program needn't handle non-finite values. No bound on the sum of `pair_count` on one device may be relied on, other than what follows from the above.
Results may differ from a plain program's by a relative error of at most 0.0003.
Values sent between devices are 32-bit elements; how exact they have to be, the bound alone decides.
A program may use at most 64 MiB of HBM per device.

v0:
```python
import functools
import math

import jax
import jax.numpy as jnp
from jax import lax
from jax.experimental import pallas as pl
from jax.experimental.pallas import tpu as pltpu
from jax.sharding import PartitionSpec as P

BLK = 128
HORIZON = 3.0
BOND_STIFF = 5.0
CONTACT_STIFF = 0.02
CONTACT_DAMP = 0.05
CONTACT_RANGE = 9.0
TIME_STEP = 0.5
VMEM_BYTES = 32 * 1024 * 1024
PICK_BYTES = 60 * 1024 * 1024
FAR = 100.0
BOND_UNROLL = 8
FAR_UNROLL = 4
PAIR_UNROLL = 16
GRAIN_UNROLL = 4
OWNER_UNROLL = 2
FIRST_SHARE = 6
ALL_SHARES = 8
F32 = jnp.float32
BF16 = jnp.bfloat16


def iota(shape, axis):
    return lax.broadcasted_iota(jnp.int32, shape, axis)


def split3(value):
    one = value.astype(BF16).astype(F32)
    rest = value - one
    two = rest.astype(BF16).astype(F32)
    return one, two, (rest - two).astype(BF16).astype(F32)


def left_rows(value):
    one, two, three = split3(value)
    return jnp.concatenate([one, one, two, one, three, two], axis=0).astype(BF16)


def right_rows(value):
    one, two, three = split3(value)
    return jnp.concatenate([one, two, one, three, one, two], axis=0).astype(BF16)


def dot(left, right, left_dim, right_dim):
    return lax.dot_general(
        left, right, (((left_dim,), (right_dim,)), ((), ())), preferred_element_type=F32
    )


def split2(value):
    high = value.astype(BF16)
    return high, (value - high.astype(F32)).astype(BF16)


def stack_rows(pieces, width, kind=F32):
    row = iota((8, width), 0)
    total = jnp.zeros((8, width), kind)
    for number, piece in pieces.items():
        total = jnp.where(row == number, jnp.broadcast_to(piece, (8, width)), total)
    return total


def lattice_row(node):
    return (
        (node % 8).astype(F32) - 3.5,
        (node // 8 % 8).astype(F32) - 3.5,
        (node // 64).astype(F32) - 5.5,
    )


def pick_kernel(order, shift_in, velocity_in, centers, nodes_in, out, held, shift, velocity, nodes, arrived):
    copies = [
        pltpu.make_async_copy(source, target, arrived.at[number])
        for number, (source, target) in enumerate(
            ((shift_in, shift), (velocity_in, velocity), (nodes_in, nodes))
        )
    ]
    for copy in copies:
        copy.start()
    _, grains, count = shift.shape
    surface = nodes.shape[1]
    blocks = surface // BLK
    owners = out.shape[0]
    share = out.shape[1] // 6
    scale = math.sqrt(2.0 * math.log2(math.e) / CONTACT_RANGE)
    same = iota((grains, grains), 0) == iota((grains, grains), 1)
    offsets = [
        jnp.sum(jnp.where(same, centers[c : c + 1, :], 0.0), axis=1, keepdims=True)
        for c in range(3)
    ]
    for copy in copies:
        copy.wait()
    for group in range(grains // 8):
        rows = slice(group * 8, group * 8 + 8)
        places = []
        speeds = []
        for tile in range(count // BLK):
            span = slice(tile * BLK, tile * BLK + BLK)
            rest = lattice_row(iota((8, BLK), 1) + tile * BLK)
            now = [rest[c] + shift[c, rows, span] + offsets[c][rows] for c in range(3)]
            places.append([scale * now[c] for c in range(3)])
            speeds.append(
                [
                    CONTACT_STIFF * now[c] - CONTACT_DAMP * velocity[c, rows, span]
                    for c in range(3)
                ]
            )
        for k in range(blocks):
            index = nodes[rows, k * BLK : k * BLK + BLK]
            low = index & (BLK - 1)
            high = index >> 7
            for c in range(6):
                source = places if c < 3 else speeds
                total = jnp.zeros((8, BLK), F32)
                for tile in range(count // BLK):
                    found = jnp.take_along_axis(source[tile][c % 3], low, axis=1)
                    total = jnp.where(high == tile, found, total)
                base = (c * blocks + k) * grains + group * 8
                held[base : base + 8, :] = total

    def send(d, carry):
        for cc in range(share):
            j = order[0, d * share + cc]
            row = (j % blocks) * grains + j // blocks
            for c in range(6):
                out[d, cc * 6 + c : cc * 6 + c + 1, :] = held[
                    pl.ds(row + c * blocks * grains, 1), :
                ]
        return carry

    lax.fori_loop(0, owners, send, 0)


def bond_kernel(first, grains, tiles, shift, bits, nodes, force, place, lefts, rights, sums, spots, total, inverse, square, dead, spread, fold, near, far):
    count = shift.shape[2]
    tile_count = bits.shape[1]
    surface = nodes.shape[1]
    blocks = count // BLK

    q = iota((BLK, BLK), 0)
    p = iota((BLK, BLK), 1)
    flat = (q % 8 - p % 8) ** 2 + (q // 8 % 8 - p // 8 % 8) ** 2
    for delta in range(-1, 2):
        squared = (flat + (2 * delta + q // 64 - p // 64) ** 2).astype(F32)
        kept = (squared > 0.25) & (squared <= HORIZON * HORIZON)
        square[delta + 1] = jnp.where(kept, squared, FAR)
        inverse[delta + 1] = 1.0 / jnp.sqrt(jnp.where(kept, squared, FAR))
        dead[delta + 1] = jnp.where(kept, 0, 255)
    fold[...] = jnp.where(q // 16 == p % 8, 1.0, 0.0).astype(BF16)
    spread[...] = jnp.where(iota((16, BLK), 1) % 16 == iota((16, BLK), 0), 1.0, 0.0).astype(BF16)

    rest = lattice_row(iota((1, count), 1))
    ones = jnp.ones((1, count), F32)

    def prepare_one(g):
        moved = [shift[c, pl.ds(first + g, 1), :] for c in range(3)]
        own = sum(2.0 * rest[c] * moved[c] + moved[c] * moved[c] for c in range(3))
        now = [rest[c] + moved[c] for c in range(3)]
        left = stack_rows(
            {0: moved[0], 1: moved[1], 2: moved[2], 3: rest[0], 4: rest[1], 5: rest[2], 6: own, 7: ones},
            count,
        )
        right = stack_rows(
            {
                0: -2.0 * now[0],
                1: -2.0 * now[1],
                2: -2.0 * now[2],
                3: -2.0 * moved[0],
                4: -2.0 * moved[1],
                5: -2.0 * moved[2],
                6: ones,
                7: own,
            },
            count,
        )
        spot = stack_rows({0: now[0], 1: now[1], 2: now[2], 3: ones}, count)
        left_all = left_rows(left)
        right_all = right_rows(right)
        one, two, three = split3(spot)
        sum_all = jnp.concatenate([one, two, three, jnp.zeros_like(one)], axis=0).astype(BF16)
        listed = nodes[pl.ds(first + g, 1), :]
        low = listed & (BLK - 1)
        high = listed >> 7
        position = iota((1, surface), 1)
        row = iota((8, surface), 0)
        hit = row == jnp.broadcast_to(high, (8, surface))
        within = jnp.where(hit, jnp.broadcast_to((position % BLK + 1).astype(F32), (8, surface)), 0.0)
        group = jnp.where(hit, jnp.broadcast_to((position // BLK).astype(F32), (8, surface)), 0.0)
        chosen = jnp.concatenate([within, group], axis=0).astype(BF16)
        match = jnp.where(
            iota((BLK, surface), 0) == jnp.broadcast_to(low, (BLK, surface)), 1.0, 0.0
        ).astype(BF16)
        found = dot(chosen, match, 1, 1)
        code = (found[:8] + float(BLK) * found[8:]).astype(jnp.int32)
        return left_all, right_all, sum_all, spot, code

    def prepare(n, carry):
        ready = [(n * GRAIN_UNROLL + u, prepare_one(n * GRAIN_UNROLL + u)) for u in range(GRAIN_UNROLL)]
        for g, (left_all, right_all, sum_all, spot, code) in ready:
            for h in range(blocks):
                span = slice(h * BLK, h * BLK + BLK)
                at = g * blocks + h
                lefts[at] = left_all[:, span]
                rights[at] = right_all[:, span]
                sums[at, :, :BLK] = sum_all[:, span]
                sums[at, :, BLK:] = sum_all[:, span]
                spots[at] = spot[:, span]
                total[at] = jnp.zeros((8, BLK), F32)
                place[pl.ds(h * grains + g, 1), :] = code[h : h + 1, :]
        return carry

    lax.fori_loop(0, grains // GRAIN_UNROLL, prepare, 0)

    def enlist(g, carry):
        near_held, far_held = carry
        for t in range(tile_count):
            gap = tiles[2 * t + 1, first + g] - tiles[2 * t, first + g]
            near[near_held] = g * tile_count + t
            far[far_held] = g * tile_count + t
            near_held = near_held + jnp.where((gap <= 1) & (gap >= -1), 1, 0)
            far_held = far_held + jnp.where((gap == 2) | (gap == -2), 1, 0)
        return near_held, far_held

    near_count, far_count = lax.fori_loop(0, grains, enlist, (0, 0))
    own_group = (iota((8, BLK), 1) // 16) == iota((8, BLK), 0)
    flag_all = jnp.left_shift(1, iota((BLK, BLK), 0) % 8)

    def step(n, carry):
        results = []
        for u in range(BOND_UNROLL):
            number = n * BOND_UNROLL + u
            good = number < near_count
            entry = near[jnp.where(good, number, 0)]
            g = entry // tile_count
            t = entry % tile_count
            a = tiles[2 * t, first + g]
            b = tiles[2 * t + 1, first + g]
            row_at = g * blocks + a
            col_at = g * blocks + b
            delta = b - a + 1
            excess = dot(lefts[col_at], rights[row_at], 0, 0)
            words = bits[first + g, pl.ds(t, 1), :].astype(F32)
            sorted_words = jnp.concatenate(
                [
                    jnp.where(
                        own_group,
                        jnp.broadcast_to(words[:, w * BLK : w * BLK + BLK], (8, BLK)),
                        0.0,
                    )
                    for w in range(16)
                ],
                axis=0,
            ).astype(BF16)
            turned = dot(spread[...], sorted_words, 1, 1).astype(jnp.int32)
            bond = inverse[delta] - lax.rsqrt(square[delta] + excess)
            flags = jnp.concatenate(
                [jnp.broadcast_to(turned[w : w + 1], (8, BLK)) for w in range(16)], axis=0
            )
            bond = jnp.where(((flags | dead[delta]) & flag_all) == 0, bond, 0.0)
            high, low = split2(bond)
            found = dot(sums[col_at], jnp.concatenate([high, low], axis=0), 1, 0)
            found = found[:8] + found[8:16] + found[16:24]
            gain = BOND_STIFF * (found - spots[row_at] * found[3:4])
            results.append((row_at, jnp.where(good, gain, 0.0)))
        for row_at, gain in results:
            total[row_at] = total[row_at] + gain
        return carry

    lax.fori_loop(0, (near_count + BOND_UNROLL - 1) // BOND_UNROLL, step, 0)

    lane = iota((8, BLK), 1)
    rank = iota((8, BLK), 0)
    turn = (lane % 64) // 8 == rank
    half_lane = iota((1, BLK), 1)

    def far_step(n, carry):
        results = []
        for u in range(FAR_UNROLL):
            number = n * FAR_UNROLL + u
            good = number < far_count
            entry = far[jnp.where(good, number, 0)]
            g = entry // tile_count
            t = entry % tile_count
            a = tiles[2 * t, first + g]
            b = tiles[2 * t + 1, first + g]
            row_at = g * blocks + a
            col_at = g * blocks + b
            upper = jnp.where(b > a, 1, 0)
            own_words = bits[first + g, pl.ds(t, 1), pl.ds(pl.multiple_of(upper * 1024, 1024), 1024)]
            words = stack_rows(
                {r: own_words[:, r * BLK : r * BLK + BLK] for r in range(8)}, BLK, jnp.int32
            )
            flags = jnp.right_shift(words, lane // 16) & 1
            flags = jnp.where(lane % 16 == rank + 8 * (1 - upper), flags, 0).astype(F32)
            flags = jnp.concatenate([flags, jnp.zeros_like(flags)], axis=0).astype(BF16)
            flags = dot(flags, fold[...], 1, 0)[:8]
            broken = jnp.sum(jnp.where(turn, flags, 0.0), axis=0, keepdims=True)
            gap = pltpu.roll(spots[col_at], 64, 1) - spots[row_at]
            squares = gap * gap
            now_square = squares[0:1] + squares[1:2] + squares[2:3]
            bond = 1.0 / HORIZON - lax.rsqrt(now_square)
            kept = (half_lane // 64 == upper) & (broken < 0.5) & good
            bond = jnp.where(kept, BOND_STIFF * bond, 0.0)
            results.append((row_at, gap * bond))
        for row_at, gain in results:
            total[row_at] = total[row_at] + gain
        return carry

    lax.fori_loop(0, (far_count + FAR_UNROLL - 1) // FAR_UNROLL, far_step, 0)

    def finish(g, carry):
        for h in range(blocks):
            for c in range(3):
                force[pl.ds((c * blocks + h) * grains + g, 1), :] = total[g * blocks + h, c : c + 1, :]
        return carry

    lax.fori_loop(0, grains, finish, 0)


def contact_kernel(pairs, count, received, out, lefts, rights, sums, total):
    owners = received.shape[0]
    share = received.shape[1] // 6

    def prepare(n, carry):
        for u in range(OWNER_UNROLL * share):
            at = n * OWNER_UNROLL * share + u
            s = n * OWNER_UNROLL + u // share
            cc = u % share
            line = [received[s, cc * 6 + c : cc * 6 + c + 1, :] for c in range(6)]
            own = -0.5 * (line[0] * line[0] + line[1] * line[1] + line[2] * line[2])
            one = jnp.ones((1, BLK), F32)
            base = {0: line[0], 1: line[1], 2: line[2]}
            lefts[at] = left_rows(stack_rows({**base, 3: own, 4: one}, BLK))
            rights[at] = right_rows(stack_rows({**base, 3: one, 4: own}, BLK))
            first, second, _ = split3(stack_rows({0: line[3], 1: line[4], 2: line[5], 3: one}, BLK))
            both = jnp.concatenate([first, second], axis=0).astype(BF16)
            sums[at, :, :BLK] = both
            sums[at, :, BLK:] = both
            total[at] = jnp.zeros((8, BLK), F32)
        return carry

    lax.fori_loop(0, owners // OWNER_UNROLL, prepare, 0)
    live = count[0]

    def step(n, carry):
        results = []
        for u in range(PAIR_UNROLL):
            number = n * PAIR_UNROLL + u
            good = number < live
            at = jnp.where(good, number, 0)
            i = pairs[0, at]
            j = pairs[1, at]
            weight = jnp.exp2(dot(lefts[j], rights[i], 0, 0))
            high, low = split2(weight)
            gain_i = dot(sums[j], jnp.concatenate([high, low], axis=0), 1, 0)
            gain_j = dot(sums[i], jnp.concatenate([high, low], axis=1), 1, 1)
            results.append((i, jnp.where(good, gain_i[:8] + gain_i[8:], 0.0)))
            results.append((j, jnp.where(good, gain_j[:8] + gain_j[8:], 0.0)))
        for at, gain in results:
            total[at] = total[at] + gain
        return carry

    lax.fori_loop(0, (live + PAIR_UNROLL - 1) // PAIR_UNROLL, step, 0)

    def finish(s, carry):
        for cc in range(share):
            found = total[s * share + cc]
            weight = found[3:4]
            for c in range(3):
                out[s, cc * 3 + c : cc * 3 + c + 1, :] = (
                    received[s, cc * 6 + 3 + c : cc * 6 + 4 + c, :] * weight - found[c : c + 1]
                )
        return carry

    lax.fori_loop(0, owners, finish, 0)


def finish_kernel(cut, order, returned, place_a, bond_a, place_b, bond_b, velocity, force, speed, held):
    _, grains, count = velocity.shape
    owners = returned.shape[0]
    node_blocks = count // BLK
    share = returned.shape[1] // 3
    blocks = held.shape[0] // (3 * grains)

    def accept(d, carry):
        for cc in range(share):
            j = order[0, d * share + cc]
            row = (j % blocks) * grains + j // blocks
            for c in range(3):
                held[pl.ds(row + c * blocks * grains, 1), :] = returned[
                    d, cc * 3 + c : cc * 3 + c + 1, :
                ]
        return carry

    lax.fori_loop(0, owners, accept, 0)
    for group in range(grains // 8):
        rows = slice(group * 8, group * 8 + 8)
        for tile in range(count // BLK):
            span = slice(tile * BLK, tile * BLK + BLK)
            early = group * 8 < cut
            place, bond = (place_a, bond_a) if early else (place_b, bond_b)
            part = cut if early else grains - cut
            own = group * 8 - (0 if early else cut)
            base = tile * part + own
            code = place[base : base + 8, :]
            spot = code - 1
            low = spot & (BLK - 1)
            high = jnp.where(code == 0, -1, spot >> 7)
            for c in range(3):
                total = jnp.zeros((8, BLK), F32)
                for k in range(blocks):
                    at = (c * blocks + k) * grains + group * 8
                    found = jnp.take_along_axis(held[at : at + 8, :], low, axis=1)
                    total = jnp.where(high == k, found, total)
                near = (c * node_blocks + tile) * part + own
                total = bond[near : near + 8, :] + total
                force[c, rows, span] = total
                speed[c, rows, span] = velocity[c, rows, span] + TIME_STEP * total


def on_device(displacement, velocity, centers, tile_list, broken_bits, surface_nodes, send_order, pair_list, pair_count):
    grains, _, count = displacement.shape
    owners = lax.axis_size("grain") * lax.axis_size("cell")
    slots = send_order.shape[1]
    share = slots // owners
    surface = surface_nodes.shape[1]
    blocks = surface // BLK
    node_blocks = count // BLK
    tile_count = tile_list.shape[1]
    shift = displacement.transpose(1, 0, 2)
    speed = velocity.transpose(1, 0, 2)
    tiles = tile_list.transpose(1, 2, 0).reshape(2 * tile_count, grains)
    pairs = pair_list[0].T
    vmem = pl.BlockSpec(memory_space=pltpu.VMEM)
    smem = pl.BlockSpec(memory_space=pltpu.SMEM)
    hbm = pl.BlockSpec(memory_space=pltpu.HBM)
    params = pltpu.CompilerParams(vmem_limit_bytes=VMEM_BYTES)

    outgoing = pl.pallas_call(
        pick_kernel,
        out_shape=jax.ShapeDtypeStruct((owners, 6 * share, BLK), F32),
        in_specs=[smem, hbm, hbm, vmem, hbm],
        out_specs=vmem,
        scratch_shapes=[
            pltpu.VMEM((6 * slots, BLK), F32),
            pltpu.VMEM((3, grains, count), F32),
            pltpu.VMEM((3, grains, count), F32),
            pltpu.VMEM((grains, surface), jnp.int32),
            pltpu.SemaphoreType.DMA((3,)),
        ],
        compiler_params=pltpu.CompilerParams(vmem_limit_bytes=PICK_BYTES),
        name="pick",
    )(send_order, shift, speed, centers, surface_nodes)

    def bonds(first, part, shift_now):
        return pl.pallas_call(
            functools.partial(bond_kernel, first, part),
            out_shape=(
                jax.ShapeDtypeStruct((3 * node_blocks * part, BLK), F32),
                jax.ShapeDtypeStruct((node_blocks * part, BLK), jnp.int32),
            ),
            in_specs=[smem, vmem, vmem, vmem],
            out_specs=(vmem, vmem),
            scratch_shapes=[
                pltpu.VMEM((part * node_blocks, 48, BLK), BF16),
                pltpu.VMEM((part * node_blocks, 48, BLK), BF16),
                pltpu.VMEM((part * node_blocks, 32, 2 * BLK), BF16),
                pltpu.VMEM((part * node_blocks, 8, BLK), F32),
                pltpu.VMEM((part * node_blocks, 8, BLK), F32),
                pltpu.VMEM((3, BLK, BLK), F32),
                pltpu.VMEM((3, BLK, BLK), F32),
                pltpu.VMEM((3, BLK, BLK), jnp.int32),
                pltpu.VMEM((16, BLK), BF16),
                pltpu.VMEM((BLK, BLK), BF16),
                pltpu.SMEM((part * tile_count + 1,), jnp.int32),
                pltpu.SMEM((part * tile_count + 1,), jnp.int32),
            ],
            compiler_params=params,
            cost_estimate=pl.CostEstimate(
                flops=4_000_000_000, bytes_accessed=3_000_000, transcendentals=4_000_000
            ),
            name="bond",
        )(tiles, shift_now, broken_bits, surface_nodes)

    cut = grains * FIRST_SHARE // ALL_SHARES // 8 * 8
    outgoing, shift_now = lax.optimization_barrier((outgoing, shift))
    received = lax.all_to_all(outgoing, ("grain", "cell"), split_axis=0, concat_axis=0, tiled=True)
    bond_a, place_a = bonds(0, cut, shift_now)
    received, bond_a, place_a = lax.optimization_barrier((received, bond_a, place_a))

    slot_force = pl.pallas_call(
        contact_kernel,
        out_shape=jax.ShapeDtypeStruct((owners, 3 * share, BLK), F32),
        in_specs=[smem, smem, vmem],
        out_specs=vmem,
        scratch_shapes=[
            pltpu.VMEM((slots, 48, BLK), BF16),
            pltpu.VMEM((slots, 48, BLK), BF16),
            pltpu.VMEM((slots, 16, 2 * BLK), BF16),
            pltpu.VMEM((slots, 8, BLK), F32),
        ],
        compiler_params=params,
        name="contact",
    )(pairs, pair_count, received)

    slot_force, shift_now = lax.optimization_barrier((slot_force, shift_now))
    returned = lax.all_to_all(slot_force, ("grain", "cell"), split_axis=0, concat_axis=0, tiled=True)
    bond_b, place_b = bonds(cut, grains - cut, shift_now)

    force, new_speed = pl.pallas_call(
        functools.partial(finish_kernel, cut),
        out_shape=(jax.ShapeDtypeStruct((3, grains, count), F32),) * 2,
        in_specs=[smem, vmem, vmem, vmem, vmem, vmem, vmem],
        out_specs=(vmem, vmem),
        scratch_shapes=[pltpu.VMEM((3 * slots, BLK), F32)],
        compiler_params=params,
        name="finish",
    )(send_order, returned, place_a, bond_a, place_b, bond_b, speed)
    return force.transpose(1, 0, 2), new_speed.transpose(1, 0, 2)


def solution(mesh):
    own = ("grain", "cell")
    return jax.shard_map(
        on_device,
        mesh=mesh,
        in_specs=(
            P(own, None, None),
            P(own, None, None),
            P(None, own),
            P(own, None, None),
            P(own, None, None),
            P(own, None),
            P(own, None),
            P(own, None, None),
            P(own),
        ),
        out_specs=(P(own, None, None), P(own, None, None)),
        check_vma=False,
    )
```

profile of v0, /device:TPU:1, one launch (start us, length us, event | category | flops | bytes accessed | tf_op | source)
XLA Modules:
  0.0 66.5 jit_solution(12666676747298185010)
XLA Ops:
  0.6 0.0 copy-start.5
  0.6 4.4 %pick.1 = f32[32,24,128]{2,1,0:T(8,128)} custom-call(s32[1,128]{1,0:T(1,128)} %order.3, f32[3,32,768]{2,1,0:T(8,128)} %bitcast.12, f32[3,32,768]{2,1,0:T(8,128)} %bitcast.10, f32[3,32]{1,0:T(4,128)} %centers.1, s32[32,512]{1,0:T(8,128)} %nodes.3), custom_call_target="tpu_custom_call" | custom-call | tf_op jit(solution)/shard_map/pick/pallas_call | solution.py:448
  5.0 0.0 copy-start.1
  5.1 0.0 copy-start.2
  5.1 0.0 copy-start.6
  5.1 7.1 %all-to-all-start = ((f32[32,24,128]{2,1,0:T(8,128)}), f32[32,24,128]{2,1,0:T(8,128)S(1)}, u32[]{:S(2)}, u32[]{:S(2)}) async-start(f32[32,24,128]{2,1,0:T(8,128)} %pick.1), calls=%async_computation | async-start | bytes 786432 | tf_op jit(solution)/shard_map/all_to_all | solution.py:496
  12.8 0.0 copy-done.5
  12.9 0.0 copy-done.1
  12.9 0.0 copy-done.2
  12.9 0.0 copy-done.6
  12.9 16.2 %bond.2 = (f32[432,128]{1,0:T(8,128)S(1)}, s32[144,128]{1,0:T(8,128)S(1)}) custom-call(s32[8,32]{1,0:T(8,128)S(1)} %bitcast.16, f32[3,32,768]{2,1,0:T(8,128)S(1)} %bitcast.13, s32[32,4,2048]{2,1,0:T(4,128)S(1)} %copy-done.5, s32[32,512]{1,0:T(8,128)S(1)} %copy-done.2), custom_call_target="tpu_custom_call" | custom-call | flops 4000000000 | bytes 3000000 | tf_op jit(solution)/shard_map/bond/pallas_call | solution.py:465
  29.1 0.0 all-to-all-done.received
  29.1 0.0 copy-start.4
  29.1 0.7 %copy-done.4 = s32[1,128,2]{1,2,0:T(2,128)S(1)} copy-done((s32[1,128,2]{1,2,0:T(2,128)S(1)}, s32[1,128,2]{1,2,0:T(2,128)}, u32[]{:S(2)}) %copy-start.4) | copy-done | bytes 1048
  29.8 4.2 %contact.1 = f32[32,12,128]{2,1,0:T(8,128)} custom-call(s32[2,128]{1,0:T(2,128)S(1)} %bitcast.15, s32[1]{0:T(128)S(6)} %copy.11.count, f32[32,24,128]{2,1,0:T(8,128)S(1)} %all-to-all-done.received), custom_call_target="tpu_custom_call" | custom-call | tf_op jit(solution)/shard_map/contact/pallas_call | solution.py:500
  34.0 18.8 %all-to-all-start.1 = ((f32[32,12,128]{2,1,0:T(8,128)}), f32[32,12,128]{2,1,0:T(8,128)S(1)}, u32[]{:S(2)}, u32[]{:S(2)}) async-start(f32[32,12,128]{2,1,0:T(8,128)} %contact.1), calls=%async_computation.1 | async-start | bytes 524288 | tf_op jit(solution)/shard_map/all_to_all | solution.py:516
  52.7 0.0 copy-start
  52.7 7.4 %bond.3 = (f32[144,128]{1,0:T(8,128)S(1)}, s32[48,128]{1,0:T(8,128)S(1)}) custom-call(s32[8,32]{1,0:T(8,128)S(1)} %bitcast.17, f32[3,32,768]{2,1,0:T(8,128)S(1)} %bitcast.14, s32[32,4,2048]{2,1,0:T(4,128)S(1)} %copy-done.5, s32[32,512]{1,0:T(8,128)S(1)} %copy-done.2), custom_call_target="tpu_custom_call" | custom-call | flops 4000000000 | bytes 3000000 | tf_op jit(solution)/shard_map/bond/pallas_call | solution.py:465
  60.2 2.8 %all-to-all-done.1.returned = f32[32,12,128]{2,1,0:T(8,128)S(1)} async-done(((f32[32,12,128]{2,1,0:T(8,128)}), f32[32,12,128]{2,1,0:T(8,128)S(1)}, u32[]{:S(2)}, u32[]{:S(2)}) %all-to-all-start.1) | async-done | bytes 196640 | tf_op jit(solution)/shard_map/all_to_all | solution.py:516
  63.0 0.0 copy-start.3
  63.0 0.0 copy-done
  63.0 0.7 copy-done.3
  63.6 2.8 %finish.1 = (f32[3,32,768]{2,1,0:T(8,128)}, f32[3,32,768]{2,1,0:T(8,128)}) custom-call(s32[1,128]{1,0:T(1,128)S(1)} %copy-done.3, f32[32,12,128]{2,1,0:T(8,128)S(1)} %all-to-all-done.1.returned, s32[144,128]{1,0:T(8,128)S(1)} %get-tuple-element.21.place_a, f32[432,128]{1,0:T(8,128)S(1)} %get-tuple-element.22.bond_a, ...), custom_call_target="tpu_custom_call" | custom-call | tf_op jit(solution)/shard_map/finish/pallas_call | solution.py:519
Async XLA Ops:
  0.6 12.2 %copy-start.5 = (s32[32,4,2048]{2,1,0:T(4,128)S(1)}, s32[32,4,2048]{2,1,0:T(4,128)}, u32[]{:S(2)}) copy-start(s32[32,4,2048]{2,1,0:T(4,128)} %bits.3) | copy-start | bytes 3145732
  5.0 7.8 %copy-start.1 = (f32[32,3,768]{2,0,1:T(8,128)S(1)}, f32[32,3,768]{2,0,1:T(8,128)}, u32[]{:S(2)}) copy-start(f32[32,3,768]{2,0,1:T(8,128)} %param.9) | copy-start | bytes 884740
  5.1 7.8 %copy-start.2 = (s32[32,512]{1,0:T(8,128)S(1)}, s32[32,512]{1,0:T(8,128)}, u32[]{:S(2)}) copy-start(s32[32,512]{1,0:T(8,128)} %nodes.3) | copy-start | bytes 196612
  5.1 7.8 %copy-start.6 = (s32[32,4,2]{0,2,1:T(2,128)S(1)}, s32[32,4,2]{0,2,1:T(2,128)}, u32[]{:S(2)}) copy-start(s32[32,4,2]{0,2,1:T(2,128)} %param.12) | copy-start | bytes 3076
  5.1 24.0 %all-to-all-start = ((f32[32,24,128]{2,1,0:T(8,128)}), f32[32,24,128]{2,1,0:T(8,128)S(1)}, u32[]{:S(2)}, u32[]{:S(2)}) async-start(f32[32,24,128]{2,1,0:T(8,128)} %pick.1), calls=%async_computation | async-start | bytes 786432 | tf_op jit(solution)/shard_map/all_to_all | solution.py:496
  29.1 0.7 %copy-start.4 = (s32[1,128,2]{1,2,0:T(2,128)S(1)}, s32[1,128,2]{1,2,0:T(2,128)}, u32[]{:S(2)}) copy-start(s32[1,128,2]{1,2,0:T(2,128)} %param.16) | copy-start | bytes 3076
  34.0 29.0 %all-to-all-start.1 = ((f32[32,12,128]{2,1,0:T(8,128)}), f32[32,12,128]{2,1,0:T(8,128)S(1)}, u32[]{:S(2)}, u32[]{:S(2)}) async-start(f32[32,12,128]{2,1,0:T(8,128)} %contact.1), calls=%async_computation.1 | async-start | bytes 524288 | tf_op jit(solution)/shard_map/all_to_all | solution.py:516
  52.7 10.3 %copy-start = (f32[32,3,768]{2,0,1:T(8,128)S(1)}, f32[32,3,768]{2,0,1:T(8,128)}, u32[]{:S(2)}) copy-start(f32[32,3,768]{2,0,1:T(8,128)} %param.10) | copy-start | bytes 884740
  63.0 0.7 copy-start.3
where the time goes:
time: 67.7 us; the launch traced here: 66.5 us
  Pallas kernels  35 us (52%)
  starting transfers between devices  25.9 us (38%)
  waiting for transfers between devices  2.82 us (4%)
  between operations  1.41 us (2%)
  local copies, waits for them, and re-layouts  1.36 us (2%)
    pallas_call x2, Pallas kernels, bonds(): pl.pallas_call(functools.partial(bond_kernel, first, part), out_shape=(ja...  23.6 us
    all_to_all x1, starting transfers between devices, on_device(): lax.all_to_all(slot_force, ('grain', 'cell'), split_axis=0, concat_axis=0...  18.8 us
    all_to_all x1, starting transfers between devices, on_device(): lax.all_to_all(outgoing, ('grain', 'cell'), split_axis=0, concat_axis=0,...  7.1 us
    pallas_call x1, Pallas kernels, on_device(): pl.pallas_call(pick_kernel, out_shape=jax.ShapeDtypeStruct((owners, 6 * s...  4.4 us
    pallas_call x1, Pallas kernels, on_device(): pl.pallas_call(contact_kernel, out_shape=jax.ShapeDtypeStruct((owners, 3...  4.2 us
    all_to_all x1, waiting for transfers between devices, on_device(): lax.all_to_all(slot_force, ('grain', 'cell'), split_axis=0, concat_axis=0...  2.82 us
    pallas_call x1, Pallas kernels, on_device(): pl.pallas_call(functools.partial(finish_kernel, cut), out_shape=(jax.Shap...  2.81 us
    unnamed x14, local copies, waits for them, and re-layouts  1.36 us
  transfers between devices with their start and end apart: 2, of which 1 were waited for; matrix products, arithmetic and copies ran while one was open for 0% of the time, Pallas kernels for 36%

commit v1 on v0

--- a/solution.py
+++ b/solution.py
@@ -140,7 +140,12 @@
     lax.fori_loop(0, owners, send, 0)
 
 
-def bond_kernel(first, grains, tiles, shift, bits, nodes, force, place, lefts, rights, sums, spots, total, inverse, square, dead, spread, fold, near, far):
+def bond_kernel(first, grains, tiles, shift, bits, nodes, *refs):
+    handed = (len(refs) - 15) // 2
+    for listing, listing_out in zip(refs[:handed], refs[handed + 2 :]):
+        listing_out[...] = listing[...]
+    force, place = refs[handed : handed + 2]
+    lefts, rights, sums, spots, total, inverse, square, dead, spread, fold, fixed, near, far = refs[-13:]
     count = shift.shape[2]
     tile_count = bits.shape[1]
     surface = nodes.shape[1]
@@ -158,47 +163,46 @@
     fold[...] = jnp.where(q // 16 == p % 8, 1.0, 0.0).astype(BF16)
     spread[...] = jnp.where(iota((16, BLK), 1) % 16 == iota((16, BLK), 0), 1.0, 0.0).astype(BF16)
 
-    rest = lattice_row(iota((1, count), 1))
-    ones = jnp.ones((1, count), F32)
+    wide = (8, count)
+    row = iota(wide, 0)
+    rest = lattice_row(iota(wide, 1))
+    rest_rows = jnp.where(row == 0, rest[0], jnp.where(row == 1, rest[1], jnp.where(row == 2, rest[2], 0.0)))
+    fixed[0] = rest_rows
+    fixed[1] = pltpu.roll(rest_rows, 3, 0) + jnp.where(row == 7, 1.0, 0.0)
+    fixed[2] = rest_rows - jnp.where(row == 6, 0.5, 0.0)
+    fixed[3] = rest_rows + jnp.where(row == 3, 1.0, 0.0)
+    ids = iota((BLK, BLK), 0).astype(F32).astype(BF16)
 
     def prepare_one(g):
-        moved = [shift[c, pl.ds(first + g, 1), :] for c in range(3)]
-        own = sum(2.0 * rest[c] * moved[c] + moved[c] * moved[c] for c in range(3))
-        now = [rest[c] + moved[c] for c in range(3)]
-        left = stack_rows(
-            {0: moved[0], 1: moved[1], 2: moved[2], 3: rest[0], 4: rest[1], 5: rest[2], 6: own, 7: ones},
-            count,
-        )
-        right = stack_rows(
-            {
-                0: -2.0 * now[0],
-                1: -2.0 * now[1],
-                2: -2.0 * now[2],
-                3: -2.0 * moved[0],
-                4: -2.0 * moved[1],
-                5: -2.0 * moved[2],
-                6: ones,
-                7: own,
-            },
-            count,
-        )
-        spot = stack_rows({0: now[0], 1: now[1], 2: now[2], 3: ones}, count)
+        moved = stack_rows({c: shift[c, pl.ds(first + g, 1), :] for c in range(3)}, count)
+        own = jnp.sum(moved * (moved + 2.0 * fixed[0]), axis=0, keepdims=True)
+        left = jnp.where(row == 6, own, moved + fixed[1])
+        right = jnp.where(row == 7, own, -2.0 * (moved + pltpu.roll(moved, 3, 0) + fixed[2]))
+        spot = moved + fixed[3]
         left_all = left_rows(left)
         right_all = right_rows(right)
         one, two, three = split3(spot)
         sum_all = jnp.concatenate([one, two, three, jnp.zeros_like(one)], axis=0).astype(BF16)
+
         listed = nodes[pl.ds(first + g, 1), :]
-        low = listed & (BLK - 1)
+        low = (listed & (BLK - 1)).astype(F32).astype(BF16)
         high = listed >> 7
         position = iota((1, surface), 1)
-        row = iota((8, surface), 0)
-        hit = row == jnp.broadcast_to(high, (8, surface))
+        hit = iota((8, surface), 0) == jnp.broadcast_to(high, (8, surface))
         within = jnp.where(hit, jnp.broadcast_to((position % BLK + 1).astype(F32), (8, surface)), 0.0)
         group = jnp.where(hit, jnp.broadcast_to((position // BLK).astype(F32), (8, surface)), 0.0)
         chosen = jnp.concatenate([within, group], axis=0).astype(BF16)
-        match = jnp.where(
-            iota((BLK, surface), 0) == jnp.broadcast_to(low, (BLK, surface)), 1.0, 0.0
-        ).astype(BF16)
+        match = jnp.concatenate(
+            [
+                jnp.where(
+                    ids == jnp.broadcast_to(low[:, k * BLK : k * BLK + BLK], (BLK, BLK)),
+                    jnp.ones((BLK, BLK), BF16),
+                    jnp.zeros((BLK, BLK), BF16),
+                )
+                for k in range(surface // BLK)
+            ],
+            axis=1,
+        )
         found = dot(chosen, match, 1, 1)
         code = (found[:8] + float(BLK) * found[8:]).astype(jnp.int32)
         return left_all, right_all, sum_all, spot, code
@@ -329,20 +333,23 @@
 def contact_kernel(pairs, count, received, out, lefts, rights, sums, total):
     owners = received.shape[0]
     share = received.shape[1] // 6
+    row = iota((8, BLK), 0)
+    third = jnp.where(row == 3, 1.0, 0.0)
+    fourth = jnp.where(row == 4, 1.0, 0.0)
 
     def prepare(n, carry):
         for u in range(OWNER_UNROLL * share):
             at = n * OWNER_UNROLL * share + u
             s = n * OWNER_UNROLL + u // share
             cc = u % share
-            line = [received[s, cc * 6 + c : cc * 6 + c + 1, :] for c in range(6)]
-            own = -0.5 * (line[0] * line[0] + line[1] * line[1] + line[2] * line[2])
-            one = jnp.ones((1, BLK), F32)
-            base = {0: line[0], 1: line[1], 2: line[2]}
-            lefts[at] = left_rows(stack_rows({**base, 3: own, 4: one}, BLK))
-            rights[at] = right_rows(stack_rows({**base, 3: one, 4: own}, BLK))
-            first, second, _ = split3(stack_rows({0: line[3], 1: line[4], 2: line[5], 3: one}, BLK))
-            both = jnp.concatenate([first, second], axis=0).astype(BF16)
+            line = received[s, cc * 6 : cc * 6 + 6, :]
+            line = jnp.concatenate([line, jnp.zeros((2, BLK), F32)], axis=0)
+            place = jnp.where(row < 3, line, 0.0)
+            own = -0.5 * jnp.sum(place * place, axis=0, keepdims=True)
+            lefts[at] = left_rows(jnp.where(row == 3, own, place + fourth))
+            rights[at] = right_rows(jnp.where(row == 4, own, place + third))
+            high, low, _ = split3(jnp.where(row == 6, 1.0, jnp.where(row < 3, 0.0, line)))
+            both = jnp.concatenate([high, low], axis=0).astype(BF16)
             sums[at, :, :BLK] = both
             sums[at, :, BLK:] = both
             total[at] = jnp.zeros((8, BLK), F32)
@@ -374,11 +381,8 @@
     def finish(s, carry):
         for cc in range(share):
             found = total[s * share + cc]
-            weight = found[3:4]
-            for c in range(3):
-                out[s, cc * 3 + c : cc * 3 + c + 1, :] = (
-                    received[s, cc * 6 + 3 + c : cc * 6 + 4 + c, :] * weight - found[c : c + 1]
-                )
+            speeds = received[s, cc * 6 + 3 : cc * 6 + 6, :]
+            out[s, cc * 3 : cc * 3 + 3, :] = speeds * found[6:7] - found[3:6]
         return carry
 
     lax.fori_loop(0, owners, finish, 0)
@@ -461,15 +465,16 @@
         name="pick",
     )(send_order, shift, speed, centers, surface_nodes)
 
-    def bonds(first, part, shift_now):
+    def bonds(first, part, shift_now, *listings):
         return pl.pallas_call(
             functools.partial(bond_kernel, first, part),
             out_shape=(
                 jax.ShapeDtypeStruct((3 * node_blocks * part, BLK), F32),
                 jax.ShapeDtypeStruct((node_blocks * part, BLK), jnp.int32),
+                *[jax.ShapeDtypeStruct(listing.shape, jnp.int32) for listing in listings],
             ),
-            in_specs=[smem, vmem, vmem, vmem],
-            out_specs=(vmem, vmem),
+            in_specs=[smem, vmem, vmem, vmem] + [vmem] * len(listings),
+            out_specs=(vmem,) * (2 + len(listings)),
             scratch_shapes=[
                 pltpu.VMEM((part * node_blocks, 48, BLK), BF16),
                 pltpu.VMEM((part * node_blocks, 48, BLK), BF16),
@@ -481,6 +486,7 @@
                 pltpu.VMEM((3, BLK, BLK), jnp.int32),
                 pltpu.VMEM((16, BLK), BF16),
                 pltpu.VMEM((BLK, BLK), BF16),
+                pltpu.VMEM((4, 8, count), F32),
                 pltpu.SMEM((part * tile_count + 1,), jnp.int32),
                 pltpu.SMEM((part * tile_count + 1,), jnp.int32),
             ],
@@ -489,12 +495,12 @@
                 flops=4_000_000_000, bytes_accessed=3_000_000, transcendentals=4_000_000
             ),
             name="bond",
-        )(tiles, shift_now, broken_bits, surface_nodes)
+        )(tiles, shift_now, broken_bits, surface_nodes, *listings)
 
     cut = grains * FIRST_SHARE // ALL_SHARES // 8 * 8
     outgoing, shift_now = lax.optimization_barrier((outgoing, shift))
     received = lax.all_to_all(outgoing, ("grain", "cell"), split_axis=0, concat_axis=0, tiled=True)
-    bond_a, place_a = bonds(0, cut, shift_now)
+    bond_a, place_a, pairs, order = bonds(0, cut, shift_now, pairs, send_order)
     received, bond_a, place_a = lax.optimization_barrier((received, bond_a, place_a))
 
     slot_force = pl.pallas_call(
@@ -524,7 +530,7 @@
         scratch_shapes=[pltpu.VMEM((3 * slots, BLK), F32)],
         compiler_params=params,
         name="finish",
-    )(send_order, returned, place_a, bond_a, place_b, bond_b, speed)
+    )(order, returned, place_a, bond_a, place_b, bond_b, speed)
     return force.transpose(1, 0, 2), new_speed.transpose(1, 0, 2)
 
 

time: 67.7 us -> 63.9 us (0.944)
  Pallas kernels: 35 us -> 30.5 us
  waiting for transfers between devices: 2.82 us -> 4.68 us
  local copies, waits for them, and re-layouts: 1.36 us -> 0.67 us
    pallas_call x2, Pallas kernels: 23.6 us -> 19.3 us  [bonds(): pl.pallas_call(functools.partial(bond_kernel, first, part), out_shape=(ja...]
    all_to_all x1, waiting for transfers between devices: 2.82 us -> 4.68 us  [on_device(): lax.all_to_all(slot_force, ('grain', 'cell'), split_axis=0, concat_axis=0...]
    unnamed x14, local copies, waits for them, and re-layouts: 1.36 us -> 0.67 us
  transfers between devices with their start and end apart: 2 -> 2, of which waited for: 1 -> 1; matrix products, arithmetic and copies ran while one was open for 0% -> 0% of each run, Pallas kernels for 36% -> 31%
where the time goes in v1:
time: 63.9 us; the launch traced here: 63.1 us
  Pallas kernels  30.5 us (48%)
  starting transfers between devices  25.8 us (40%)
  waiting for transfers between devices  4.68 us (7%)
  between operations  1.43 us (2%)
  local copies, waits for them, and re-layouts  0.67 us (1%)
    pallas_call x2, Pallas kernels, bonds(): pl.pallas_call(functools.partial(bond_kernel, first, part), out_shape=(ja...  19.3 us
    all_to_all x1, starting transfers between devices, on_device(): lax.all_to_all(slot_force, ('grain', 'cell'), split_axis=0, concat_axis=0...  18.7 us
    all_to_all x1, starting transfers between devices, on_device(): lax.all_to_all(outgoing, ('grain', 'cell'), split_axis=0, concat_axis=0,...  7.1 us
    all_to_all x1, waiting for transfers between devices, on_device(): lax.all_to_all(slot_force, ('grain', 'cell'), split_axis=0, concat_axis=0...  4.68 us
    pallas_call x1, Pallas kernels, on_device(): pl.pallas_call(pick_kernel, out_shape=jax.ShapeDtypeStruct((owners, 6 * s...  4.4 us
    pallas_call x1, Pallas kernels, on_device(): pl.pallas_call(contact_kernel, out_shape=jax.ShapeDtypeStruct((owners, 3...  4.02 us
    pallas_call x1, Pallas kernels, on_device(): pl.pallas_call(functools.partial(finish_kernel, cut), out_shape=(jax.Shap...  2.81 us
  transfers between devices with their start and end apart: 2, of which 1 were waited for; matrix products, arithmetic and copies ran while one was open for 0% of the time, Pallas kernels for 31%

profile of v1, /device:TPU:1, one launch (start us, length us, event | category | flops | bytes accessed | tf_op | source)
XLA Modules:
  0.0 63.1 jit_solution(1342618525266943121)
XLA Ops:
  0.6 0.0 copy-start.4
  0.6 4.4 %pick.1 = f32[32,24,128]{2,1,0:T(8,128)} custom-call(s32[1,128]{1,0:T(1,128)} %refs_1_.1, f32[3,32,768]{2,1,0:T(8,128)} %bitcast.12, f32[3,32,768]{2,1,0:T(8,128)} %bitcast.10, f32[3,32]{1,0:T(4,128)} %centers.1, s32[32,512]{1,0:T(8,128)} %nodes.3), custom_call_target="tpu_custom_call" | custom-call | tf_op jit(solution)/shard_map/pick/pallas_call | solution.py:452
  5.0 0.0 copy-start.1
  5.1 0.0 copy-start.2
  5.1 7.1 %all-to-all-start = ((f32[32,24,128]{2,1,0:T(8,128)}), f32[32,24,128]{2,1,0:T(8,128)S(1)}, u32[]{:S(2)}, u32[]{:S(2)}) async-start(f32[32,24,128]{2,1,0:T(8,128)} %pick.1), calls=%async_computation | async-start | bytes 786432 | tf_op jit(solution)/shard_map/all_to_all | solution.py:502
  12.2 0.0 copy-start.5
  12.9 0.0 copy-start.3
  12.9 0.0 copy-start.6
  12.9 0.0 copy-done.4
  12.9 0.0 copy-done.1
  12.9 0.0 copy-done.2
  12.9 0.0 copy-done.5
  12.9 0.6 copy-done.3
  13.5 0.0 copy-done.6
  13.6 13.7 %bond.2 = (f32[432,128]{1,0:T(8,128)S(1)}, s32[144,128]{1,0:T(8,128)S(1)}, s32[2,128]{1,0:T(2,128)S(1)}, s32[1,128]{1,0:T(1,128)S(1)}) custom-call(s32[8,32]{1,0:T(8,128)S(1)} %bitcast.15, f32[3,32,768]{2,1,0:T(8,128)S(1)} %bitcast.13, s32[32,4,2048]{2,1,0:T(4,128)S(1)} %copy-done.4, s32[32,512]{1,0:T(8,128)S(1)} %copy-done.2, s32[2,128]{1,0:T(2,128)S(1)} %bitcast.17, ...), custom_call_target="tpu_custom_call" | custom-call | flops 4000000000 | bytes 3000000 | tf_op jit(solution)/shard_map/bond/pallas_call | solution.py:469
  27.3 0.0 all-to-all-done.received
  27.3 4.0 %contact.1 = f32[32,12,128]{2,1,0:T(8,128)} custom-call(s32[2,128]{1,0:T(2,128)S(1)} %get-tuple-element.19.pairs, s32[1]{0:T(128)S(6)} %copy.11.count, f32[32,24,128]{2,1,0:T(8,128)S(1)} %all-to-all-done.received), custom_call_target="tpu_custom_call" | custom-call | tf_op jit(solution)/shard_map/contact/pallas_call | solution.py:506
  31.3 18.7 %all-to-all-start.1 = ((f32[32,12,128]{2,1,0:T(8,128)}), f32[32,12,128]{2,1,0:T(8,128)S(1)}, u32[]{:S(2)}, u32[]{:S(2)}) async-start(f32[32,12,128]{2,1,0:T(8,128)} %contact.1), calls=%async_computation.1 | async-start | bytes 524288 | tf_op jit(solution)/shard_map/all_to_all | solution.py:522
  50.0 0.0 copy-start
  50.0 5.6 %bond.3 = (f32[144,128]{1,0:T(8,128)S(1)}, s32[48,128]{1,0:T(8,128)S(1)}) custom-call(s32[8,32]{1,0:T(8,128)S(1)} %bitcast.16, f32[3,32,768]{2,1,0:T(8,128)S(1)} %bitcast.14, s32[32,4,2048]{2,1,0:T(4,128)S(1)} %copy-done.4, s32[32,512]{1,0:T(8,128)S(1)} %copy-done.2), custom_call_target="tpu_custom_call" | custom-call | flops 4000000000 | bytes 3000000 | tf_op jit(solution)/shard_map/bond/pallas_call | solution.py:469
  55.6 4.7 %all-to-all-done.1.returned = f32[32,12,128]{2,1,0:T(8,128)S(1)} async-done(((f32[32,12,128]{2,1,0:T(8,128)}), f32[32,12,128]{2,1,0:T(8,128)S(1)}, u32[]{:S(2)}, u32[]{:S(2)}) %all-to-all-start.1) | async-done | bytes 196640 | tf_op jit(solution)/shard_map/all_to_all | solution.py:522
  60.3 0.0 copy-done
  60.3 2.8 %finish.1 = (f32[3,32,768]{2,1,0:T(8,128)}, f32[3,32,768]{2,1,0:T(8,128)}) custom-call(s32[1,128]{1,0:T(1,128)S(1)} %get-tuple-element.18.order, f32[32,12,128]{2,1,0:T(8,128)S(1)} %all-to-all-done.1.returned, s32[144,128]{1,0:T(8,128)S(1)} %get-tuple-element.25.place_a, f32[432,128]{1,0:T(8,128)S(1)} %get-tuple-element.26.bond_a, ...), custom_call_target="tpu_custom_call" | custom-call | tf_op jit(solution)/shard_map/finish/pallas_call | solution.py:525
Async XLA Ops:
  0.6 12.2 %copy-start.4 = (s32[32,4,2048]{2,1,0:T(4,128)S(1)}, s32[32,4,2048]{2,1,0:T(4,128)}, u32[]{:S(2)}) copy-start(s32[32,4,2048]{2,1,0:T(4,128)} %bits.3) | copy-start | bytes 3145732
  5.0 7.8 %copy-start.1 = (f32[32,3,768]{2,0,1:T(8,128)S(1)}, f32[32,3,768]{2,0,1:T(8,128)}, u32[]{:S(2)}) copy-start(f32[32,3,768]{2,0,1:T(8,128)} %param.9) | copy-start | bytes 884740
  5.1 7.8 %copy-start.2 = (s32[32,512]{1,0:T(8,128)S(1)}, s32[32,512]{1,0:T(8,128)}, u32[]{:S(2)}) copy-start(s32[32,512]{1,0:T(8,128)} %nodes.3) | copy-start | bytes 196612
  5.1 22.2 %all-to-all-start = ((f32[32,24,128]{2,1,0:T(8,128)}), f32[32,24,128]{2,1,0:T(8,128)S(1)}, u32[]{:S(2)}, u32[]{:S(2)}) async-start(f32[32,24,128]{2,1,0:T(8,128)} %pick.1), calls=%async_computation | async-start | bytes 786432 | tf_op jit(solution)/shard_map/all_to_all | solution.py:502
  12.2 0.7 %copy-start.5 = (s32[32,4,2]{0,2,1:T(2,128)S(1)}, s32[32,4,2]{0,2,1:T(2,128)}, u32[]{:S(2)}) copy-start(s32[32,4,2]{0,2,1:T(2,128)} %param.12) | copy-start | bytes 3076
  12.9 0.7 %copy-start.3 = (s32[1,128]{1,0:T(1,128)S(1)}, s32[1,128]{1,0:T(1,128)}, u32[]{:S(2)}) copy-start(s32[1,128]{1,0:T(1,128)} %refs_1_.1) | copy-start | bytes 1540
  12.9 0.7 %copy-start.6 = (s32[1,128,2]{1,2,0:T(2,128)S(1)}, s32[1,128,2]{1,2,0:T(2,128)}, u32[]{:S(2)}) copy-start(s32[1,128,2]{1,2,0:T(2,128)} %param.16) | copy-start | bytes 3076
  31.3 29.0 %all-to-all-start.1 = ((f32[32,12,128]{2,1,0:T(8,128)}), f32[32,12,128]{2,1,0:T(8,128)S(1)}, u32[]{:S(2)}, u32[]{:S(2)}) async-start(f32[32,12,128]{2,1,0:T(8,128)} %contact.1), calls=%async_computation.1 | async-start | bytes 524288 | tf_op jit(solution)/shard_map/all_to_all | solution.py:522
  50.0 10.3 %copy-start = (f32[32,3,768]{2,0,1:T(8,128)S(1)}, f32[32,3,768]{2,0,1:T(8,128)}, u32[]{:S(2)}) copy-start(f32[32,3,768]{2,0,1:T(8,128)} %param.10) | copy-start | bytes 884740

commit v2 on v1

--- a/solution.py
+++ b/solution.py
@@ -23,7 +23,7 @@
 PAIR_UNROLL = 16
 GRAIN_UNROLL = 4
 OWNER_UNROLL = 2
-FIRST_SHARE = 6
+FIRST_SHARE = 5
 ALL_SHARES = 8
 F32 = jnp.float32
 BF16 = jnp.bfloat16
@@ -239,7 +239,7 @@
     flag_all = jnp.left_shift(1, iota((BLK, BLK), 0) % 8)
 
     def step(n, carry):
-        results = []
+        entries = []
         for u in range(BOND_UNROLL):
             number = n * BOND_UNROLL + u
             good = number < near_count
@@ -248,33 +248,35 @@
             t = entry % tile_count
             a = tiles[2 * t, first + g]
             b = tiles[2 * t + 1, first + g]
-            row_at = g * blocks + a
-            col_at = g * blocks + b
-            delta = b - a + 1
+            entries.append((good, g, t, g * blocks + a, g * blocks + b, b - a + 1))
+        sorted_words = []
+        for _, g, t, *_ in entries:
+            words = bits[first + g, pl.ds(t, 1), :].astype(F32)
+            for w in range(16):
+                spread_row = jnp.broadcast_to(words[:, w * BLK : w * BLK + BLK], (8, BLK))
+                sorted_words.append(jnp.where(own_group, spread_row, 0.0))
+        sorted_words = jnp.concatenate(sorted_words, axis=0).astype(BF16)
+        turned = dot(spread[...], sorted_words, 1, 1).astype(jnp.int32)
+        halves = []
+        for u, (_, _, _, row_at, col_at, delta) in enumerate(entries):
             excess = dot(lefts[col_at], rights[row_at], 0, 0)
-            words = bits[first + g, pl.ds(t, 1), :].astype(F32)
-            sorted_words = jnp.concatenate(
-                [
-                    jnp.where(
-                        own_group,
-                        jnp.broadcast_to(words[:, w * BLK : w * BLK + BLK], (8, BLK)),
-                        0.0,
-                    )
-                    for w in range(16)
-                ],
-                axis=0,
-            ).astype(BF16)
-            turned = dot(spread[...], sorted_words, 1, 1).astype(jnp.int32)
             bond = inverse[delta] - lax.rsqrt(square[delta] + excess)
+            own_flags = turned[:, u * BLK : u * BLK + BLK]
             flags = jnp.concatenate(
-                [jnp.broadcast_to(turned[w : w + 1], (8, BLK)) for w in range(16)], axis=0
+                [jnp.broadcast_to(own_flags[w : w + 1], (8, BLK)) for w in range(16)], axis=0
             )
             bond = jnp.where(((flags | dead[delta]) & flag_all) == 0, bond, 0.0)
-            high, low = split2(bond)
-            found = dot(sums[col_at], jnp.concatenate([high, low], axis=0), 1, 0)
-            found = found[:8] + found[8:16] + found[16:24]
-            gain = BOND_STIFF * (found - spots[row_at] * found[3:4])
-            results.append((row_at, jnp.where(good, gain, 0.0)))
+            halves.append(jnp.concatenate(split2(bond), axis=0))
+        results = []
+        for u in range(0, BOND_UNROLL, 2):
+            left = jnp.concatenate([sums[entries[v][4]] for v in (u, u + 1)], axis=0)
+            both = dot(left, jnp.concatenate(halves[u : u + 2], axis=1), 1, 0)
+            for v in range(2):
+                good, _, _, row_at, _, _ = entries[u + v]
+                found = both[v * 32 : v * 32 + 32, v * BLK : v * BLK + BLK]
+                found = found[:8] + found[8:16] + found[16:24]
+                gain = BOND_STIFF * (found - spots[row_at] * found[3:4])
+                results.append((row_at, jnp.where(good, gain, 0.0)))
         for row_at, gain in results:
             total[row_at] = total[row_at] + gain
         return carry
@@ -359,19 +361,31 @@
     live = count[0]
 
     def step(n, carry):
-        results = []
+        ready = []
         for u in range(PAIR_UNROLL):
             number = n * PAIR_UNROLL + u
             good = number < live
             at = jnp.where(good, number, 0)
             i = pairs[0, at]
             j = pairs[1, at]
-            weight = jnp.exp2(dot(lefts[j], rights[i], 0, 0))
-            high, low = split2(weight)
-            gain_i = dot(sums[j], jnp.concatenate([high, low], axis=0), 1, 0)
-            gain_j = dot(sums[i], jnp.concatenate([high, low], axis=1), 1, 1)
-            results.append((i, jnp.where(good, gain_i[:8] + gain_i[8:], 0.0)))
-            results.append((j, jnp.where(good, gain_j[:8] + gain_j[8:], 0.0)))
+            high, low = split2(jnp.exp2(dot(lefts[j], rights[i], 0, 0)))
+            ready.append((i, j, good, high, low))
+        results = []
+        for u in range(0, PAIR_UNROLL, 2):
+            two = ready[u : u + 2]
+            upright = jnp.concatenate(
+                [jnp.concatenate([high, low], axis=0) for *_, high, low in two], axis=1
+            )
+            flat = jnp.concatenate(
+                [jnp.concatenate([high, low], axis=1) for *_, high, low in two], axis=0
+            )
+            gain_i = dot(jnp.concatenate([sums[j] for _, j, *_ in two], axis=0), upright, 1, 0)
+            gain_j = dot(jnp.concatenate([sums[i] for i, *_ in two], axis=0), flat, 1, 1)
+            for v, (i, j, good, _, _) in enumerate(two):
+                span = slice(v * BLK, v * BLK + BLK)
+                for at, gain in ((i, gain_i), (j, gain_j)):
+                    gain = gain[v * 16 : v * 16 + 8, span] + gain[v * 16 + 8 : v * 16 + 16, span]
+                    results.append((at, jnp.where(good, gain, 0.0)))
         for at, gain in results:
             total[at] = total[at] + gain
         return carry
@@ -406,16 +420,22 @@
         return carry
 
     lax.fori_loop(0, owners, accept, 0)
+
+    def rows_of(early, late, group, part):
+        start, end = group * 8, group * 8 + 8
+        pieces = []
+        if start < cut:
+            pieces.append(early[part * cut + start : part * cut + min(end, cut), :])
+        if end > cut:
+            base = part * (grains - cut) - cut
+            pieces.append(late[base + max(start, cut) : base + end, :])
+        return pieces[0] if len(pieces) == 1 else jnp.concatenate(pieces, axis=0)
+
     for group in range(grains // 8):
         rows = slice(group * 8, group * 8 + 8)
         for tile in range(count // BLK):
             span = slice(tile * BLK, tile * BLK + BLK)
-            early = group * 8 < cut
-            place, bond = (place_a, bond_a) if early else (place_b, bond_b)
-            part = cut if early else grains - cut
-            own = group * 8 - (0 if early else cut)
-            base = tile * part + own
-            code = place[base : base + 8, :]
+            code = rows_of(place_a, place_b, group, tile)
             spot = code - 1
             low = spot & (BLK - 1)
             high = jnp.where(code == 0, -1, spot >> 7)
@@ -425,8 +445,7 @@
                     at = (c * blocks + k) * grains + group * 8
                     found = jnp.take_along_axis(held[at : at + 8, :], low, axis=1)
                     total = jnp.where(high == k, found, total)
-                near = (c * node_blocks + tile) * part + own
-                total = bond[near : near + 8, :] + total
+                total = rows_of(bond_a, bond_b, group, c * node_blocks + tile) + total
                 force[c, rows, span] = total
                 speed[c, rows, span] = velocity[c, rows, span] + TIME_STEP * total
 
@@ -497,7 +516,7 @@
             name="bond",
         )(tiles, shift_now, broken_bits, surface_nodes, *listings)
 
-    cut = grains * FIRST_SHARE // ALL_SHARES // 8 * 8
+    cut = grains * FIRST_SHARE // ALL_SHARES // GRAIN_UNROLL * GRAIN_UNROLL
     outgoing, shift_now = lax.optimization_barrier((outgoing, shift))
     received = lax.all_to_all(outgoing, ("grain", "cell"), split_axis=0, concat_axis=0, tiled=True)
     bond_a, place_a, pairs, order = bonds(0, cut, shift_now, pairs, send_order)

time: 63.9 us -> 50.5 us (0.79)
  starting transfers between devices: 25.8 us -> 10.5 us
  waiting for transfers between devices: 4.68 us -> 9.79 us
  Pallas kernels: 30.5 us -> 27.2 us
    all_to_all x1, starting transfers between devices: 18.7 us -> 3.4 us  [on_device(): lax.all_to_all(slot_force, ('grain', 'cell'), split_axis=0, concat_axis=0...]
    pallas_call x2, Pallas kernels: 19.3 us -> 11.5 us  [bonds(): pl.pallas_call(functools.partial(bond_kernel, first, part), out_shape=(ja...]
    pallas_call x1, Pallas kernels: 4.02 us -> 8.55 us  [on_device(): pl.pallas_call(contact_kernel, out_shape=jax.ShapeDtypeStruct((owners, 3...]
    all_to_all x1, waiting for transfers between devices: 0.01 us -> 4.1 us  [on_device(): lax.all_to_all(outgoing, ('grain', 'cell'), split_axis=0, concat_axis=0,...]
    all_to_all x1, waiting for transfers between devices: 4.68 us -> 5.7 us  [on_device(): lax.all_to_all(slot_force, ('grain', 'cell'), split_axis=0, concat_axis=0...]
  transfers between devices with their start and end apart: 2 -> 2, of which waited for: 1 -> 2; matrix products, arithmetic and copies ran while one was open for 0% -> 0% of each run, Pallas kernels for 31% -> 23%
where the time goes in v2:
time: 50.5 us; the launch traced here: 49.6 us
  Pallas kernels  27.2 us (54%)
  starting transfers between devices  10.5 us (21%)
  waiting for transfers between devices  9.79 us (19%)
  between operations  1.42 us (3%)
  local copies, waits for them, and re-layouts  0.67 us (1%)
    pallas_call x2, Pallas kernels, bonds(): pl.pallas_call(functools.partial(bond_kernel, first, part), out_shape=(ja...  11.5 us
    pallas_call x1, Pallas kernels, on_device(): pl.pallas_call(contact_kernel, out_shape=jax.ShapeDtypeStruct((owners, 3...  8.55 us
    all_to_all x1, starting transfers between devices, on_device(): lax.all_to_all(outgoing, ('grain', 'cell'), split_axis=0, concat_axis=0,...  7.1 us
    all_to_all x1, waiting for transfers between devices, on_device(): lax.all_to_all(slot_force, ('grain', 'cell'), split_axis=0, concat_axis=0...  5.7 us
    pallas_call x1, Pallas kernels, on_device(): pl.pallas_call(pick_kernel, out_shape=jax.ShapeDtypeStruct((owners, 6 * s...  4.4 us
    all_to_all x1, waiting for transfers between devices, on_device(): lax.all_to_all(outgoing, ('grain', 'cell'), split_axis=0, concat_axis=0,...  4.1 us
    all_to_all x1, starting transfers between devices, on_device(): lax.all_to_all(slot_force, ('grain', 'cell'), split_axis=0, concat_axis=0...  3.4 us
    pallas_call x1, Pallas kernels, on_device(): pl.pallas_call(functools.partial(finish_kernel, cut), out_shape=(jax.Shap...  2.81 us
  transfers between devices with their start and end apart: 2, of which 2 were waited for; matrix products, arithmetic and copies ran while one was open for 0% of the time, Pallas kernels for 23%

profile of v2, /device:TPU:1, one launch (start us, length us, event | category | flops | bytes accessed | tf_op | source)
XLA Modules:
  0.0 49.6 jit_solution(2623462865905559894)
XLA Ops:
  0.6 0.0 copy-start.4
  0.6 4.4 %pick.1 = f32[32,24,128]{2,1,0:T(8,128)} custom-call(s32[1,128]{1,0:T(1,128)} %refs_1_.1, f32[3,32,768]{2,1,0:T(8,128)} %bitcast.12, f32[3,32,768]{2,1,0:T(8,128)} %bitcast.10, f32[3,32]{1,0:T(4,128)} %centers.1, s32[32,512]{1,0:T(8,128)} %nodes.3), custom_call_target="tpu_custom_call" | custom-call | tf_op jit(solution)/shard_map/pick/pallas_call | solution.py:471
  5.0 0.0 copy-start.1
  5.1 0.0 copy-start.2
  5.1 7.1 %all-to-all-start = ((f32[32,24,128]{2,1,0:T(8,128)}), f32[32,24,128]{2,1,0:T(8,128)S(1)}, u32[]{:S(2)}, u32[]{:S(2)}) async-start(f32[32,24,128]{2,1,0:T(8,128)} %pick.1), calls=%async_computation | async-start | bytes 786432 | tf_op jit(solution)/shard_map/all_to_all | solution.py:521
  12.2 0.0 copy-start.5
  12.9 0.0 copy-start.3
  12.9 0.0 copy-start.6
  12.9 0.0 copy-done.4
  12.9 0.0 copy-done.1
  12.9 0.0 copy-done.2
  12.9 0.0 copy-done.5
  12.9 0.6 %copy-done.3 = s32[1,128]{1,0:T(1,128)S(1)} copy-done((s32[1,128]{1,0:T(1,128)S(1)}, s32[1,128]{1,0:T(1,128)}, u32[]{:S(2)}) %copy-start.3) | copy-done | bytes 536
  13.5 0.0 copy-done.6
  13.6 6.9 %bond.2 = (f32[360,128]{1,0:T(8,128)S(1)}, s32[120,128]{1,0:T(8,128)S(1)}, s32[2,128]{1,0:T(2,128)S(1)}, s32[1,128]{1,0:T(1,128)S(1)}) custom-call(s32[8,32]{1,0:T(8,128)S(1)} %bitcast.15, f32[3,32,768]{2,1,0:T(8,128)S(1)} %bitcast.13, s32[32,4,2048]{2,1,0:T(4,128)S(1)} %copy-done.4, s32[32,512]{1,0:T(8,128)S(1)} %copy-done.2, s32[2,128]{1,0:T(2,128)S(1)} %bitcast.17, ...), custom_call_target="tpu_custom_call" | custom-call | flops 4000000000 | bytes 3000000 | tf_op jit(solution)/shard_map/bond/pallas_call | solution.py:488
  20.5 4.1 %all-to-all-done.received = f32[32,24,128]{2,1,0:T(8,128)S(1)} async-done(((f32[32,24,128]{2,1,0:T(8,128)}), f32[32,24,128]{2,1,0:T(8,128)S(1)}, u32[]{:S(2)}, u32[]{:S(2)}) %all-to-all-start) | async-done | bytes 393248 | tf_op jit(solution)/shard_map/all_to_all | solution.py:521
  24.6 8.5 %contact.1 = f32[32,12,128]{2,1,0:T(8,128)} custom-call(s32[2,128]{1,0:T(2,128)S(1)} %get-tuple-element.19.pairs, s32[1]{0:T(128)S(6)} %copy.11.count, f32[32,24,128]{2,1,0:T(8,128)S(1)} %all-to-all-done.received), custom_call_target="tpu_custom_call" | custom-call | tf_op jit(solution)/shard_map/contact/pallas_call | solution.py:525
  33.1 3.4 %all-to-all-start.1 = ((f32[32,12,128]{2,1,0:T(8,128)}), f32[32,12,128]{2,1,0:T(8,128)S(1)}, u32[]{:S(2)}, u32[]{:S(2)}) async-start(f32[32,12,128]{2,1,0:T(8,128)} %contact.1), calls=%async_computation.1 | async-start | bytes 524288 | tf_op jit(solution)/shard_map/all_to_all | solution.py:541
  36.5 0.0 copy-start
  36.6 4.5 %bond.3 = (f32[216,128]{1,0:T(8,128)S(1)}, s32[72,128]{1,0:T(8,128)S(1)}) custom-call(s32[8,32]{1,0:T(8,128)S(1)} %bitcast.16, f32[3,32,768]{2,1,0:T(8,128)S(1)} %bitcast.14, s32[32,4,2048]{2,1,0:T(4,128)S(1)} %copy-done.4, s32[32,512]{1,0:T(8,128)S(1)} %copy-done.2), custom_call_target="tpu_custom_call" | custom-call | flops 4000000000 | bytes 3000000 | tf_op jit(solution)/shard_map/bond/pallas_call | solution.py:488
  41.1 5.7 %all-to-all-done.1.returned = f32[32,12,128]{2,1,0:T(8,128)S(1)} async-done(((f32[32,12,128]{2,1,0:T(8,128)}), f32[32,12,128]{2,1,0:T(8,128)S(1)}, u32[]{:S(2)}, u32[]{:S(2)}) %all-to-all-start.1) | async-done | bytes 196640 | tf_op jit(solution)/shard_map/all_to_all | solution.py:541
  46.8 0.0 copy-done
  46.8 2.8 %finish.1 = (f32[3,32,768]{2,1,0:T(8,128)}, f32[3,32,768]{2,1,0:T(8,128)}) custom-call(s32[1,128]{1,0:T(1,128)S(1)} %get-tuple-element.18.order, f32[32,12,128]{2,1,0:T(8,128)S(1)} %all-to-all-done.1.returned, s32[120,128]{1,0:T(8,128)S(1)} %get-tuple-element.25.place_a, f32[360,128]{1,0:T(8,128)S(1)} %get-tuple-element.26.bond_a, ...), custom_call_target="tpu_custom_call" | custom-call | tf_op jit(solution)/shard_map/finish/pallas_call | solution.py:544
Async XLA Ops:
  0.6 12.2 %copy-start.4 = (s32[32,4,2048]{2,1,0:T(4,128)S(1)}, s32[32,4,2048]{2,1,0:T(4,128)}, u32[]{:S(2)}) copy-start(s32[32,4,2048]{2,1,0:T(4,128)} %bits.3) | copy-start | bytes 3145732
  5.0 7.8 %copy-start.1 = (f32[32,3,768]{2,0,1:T(8,128)S(1)}, f32[32,3,768]{2,0,1:T(8,128)}, u32[]{:S(2)}) copy-start(f32[32,3,768]{2,0,1:T(8,128)} %param.9) | copy-start | bytes 884740
  5.1 7.8 %copy-start.2 = (s32[32,512]{1,0:T(8,128)S(1)}, s32[32,512]{1,0:T(8,128)}, u32[]{:S(2)}) copy-start(s32[32,512]{1,0:T(8,128)} %nodes.3) | copy-start | bytes 196612
  5.1 19.5 %all-to-all-start = ((f32[32,24,128]{2,1,0:T(8,128)}), f32[32,24,128]{2,1,0:T(8,128)S(1)}, u32[]{:S(2)}, u32[]{:S(2)}) async-start(f32[32,24,128]{2,1,0:T(8,128)} %pick.1), calls=%async_computation | async-start | bytes 786432 | tf_op jit(solution)/shard_map/all_to_all | solution.py:521
  12.2 0.7 %copy-start.5 = (s32[32,4,2]{0,2,1:T(2,128)S(1)}, s32[32,4,2]{0,2,1:T(2,128)}, u32[]{:S(2)}) copy-start(s32[32,4,2]{0,2,1:T(2,128)} %param.12) | copy-start | bytes 3076
  12.9 0.7 %copy-start.3 = (s32[1,128]{1,0:T(1,128)S(1)}, s32[1,128]{1,0:T(1,128)}, u32[]{:S(2)}) copy-start(s32[1,128]{1,0:T(1,128)} %refs_1_.1) | copy-start | bytes 1540
  12.9 0.7 %copy-start.6 = (s32[1,128,2]{1,2,0:T(2,128)S(1)}, s32[1,128,2]{1,2,0:T(2,128)}, u32[]{:S(2)}) copy-start(s32[1,128,2]{1,2,0:T(2,128)} %param.16) | copy-start | bytes 3076
  33.1 13.7 %all-to-all-start.1 = ((f32[32,12,128]{2,1,0:T(8,128)}), f32[32,12,128]{2,1,0:T(8,128)S(1)}, u32[]{:S(2)}, u32[]{:S(2)}) async-start(f32[32,12,128]{2,1,0:T(8,128)} %contact.1), calls=%async_computation.1 | async-start | bytes 524288 | tf_op jit(solution)/shard_map/all_to_all | solution.py:541
  36.5 10.3 %copy-start = (f32[32,3,768]{2,0,1:T(8,128)S(1)}, f32[32,3,768]{2,0,1:T(8,128)}, u32[]{:S(2)}) copy-start(f32[32,3,768]{2,0,1:T(8,128)} %param.10) | copy-start | bytes 884740

commit v3 on v2

--- a/solution.py
+++ b/solution.py
@@ -22,7 +22,8 @@
 FAR_UNROLL = 4
 PAIR_UNROLL = 16
 GRAIN_UNROLL = 4
-OWNER_UNROLL = 2
+ROW_UNROLL = 2
+OWNER_UNROLL = 4
 FIRST_SHARE = 5
 ALL_SHARES = 8
 F32 = jnp.float32
@@ -114,30 +115,37 @@
                     for c in range(3)
                 ]
             )
+        index = [nodes[rows, k * BLK : k * BLK + BLK] for k in range(blocks)]
+        low = [one & (BLK - 1) for one in index]
+        high = [one >> 7 for one in index]
+        found = [[jnp.zeros((8, BLK), F32)] * 6 for _ in range(blocks)]
+        for tile in range(count // BLK):
+            sources = places[tile] + speeds[tile]
+            for k in range(blocks):
+                here = high[k] == tile
+                found[k] = [
+                    jnp.where(here, jnp.take_along_axis(sources[c], low[k], axis=1), found[k][c])
+                    for c in range(6)
+                ]
         for k in range(blocks):
-            index = nodes[rows, k * BLK : k * BLK + BLK]
-            low = index & (BLK - 1)
-            high = index >> 7
             for c in range(6):
-                source = places if c < 3 else speeds
-                total = jnp.zeros((8, BLK), F32)
-                for tile in range(count // BLK):
-                    found = jnp.take_along_axis(source[tile][c % 3], low, axis=1)
-                    total = jnp.where(high == tile, found, total)
                 base = (c * blocks + k) * grains + group * 8
-                held[base : base + 8, :] = total
-
-    def send(d, carry):
-        for cc in range(share):
-            j = order[0, d * share + cc]
-            row = (j % blocks) * grains + j // blocks
-            for c in range(6):
-                out[d, cc * 6 + c : cc * 6 + c + 1, :] = held[
-                    pl.ds(row + c * blocks * grains, 1), :
-                ]
-        return carry
-
-    lax.fori_loop(0, owners, send, 0)
+                held[base : base + 8, :] = found[k][c]
+
+    def send(n, carry):
+        moved = []
+        for u in range(ROW_UNROLL):
+            d = n * ROW_UNROLL + u
+            for cc in range(share):
+                j = order[0, d * share + cc]
+                row = (j % blocks) * grains + j // blocks
+                for c in range(6):
+                    moved.append((d, cc * 6 + c, held[pl.ds(row + c * blocks * grains, 1), :]))
+        for d, at, line in moved:
+            out[d, at : at + 1, :] = line
+        return carry
+
+    lax.fori_loop(0, owners // ROW_UNROLL, send, 0)
 
 
 def bond_kernel(first, grains, tiles, shift, bits, nodes, *refs):
@@ -340,20 +348,27 @@
     fourth = jnp.where(row == 4, 1.0, 0.0)
 
     def prepare(n, carry):
-        for u in range(OWNER_UNROLL * share):
-            at = n * OWNER_UNROLL * share + u
-            s = n * OWNER_UNROLL + u // share
-            cc = u % share
-            line = received[s, cc * 6 : cc * 6 + 6, :]
-            line = jnp.concatenate([line, jnp.zeros((2, BLK), F32)], axis=0)
-            place = jnp.where(row < 3, line, 0.0)
-            own = -0.5 * jnp.sum(place * place, axis=0, keepdims=True)
-            lefts[at] = left_rows(jnp.where(row == 3, own, place + fourth))
-            rights[at] = right_rows(jnp.where(row == 4, own, place + third))
-            high, low, _ = split3(jnp.where(row == 6, 1.0, jnp.where(row < 3, 0.0, line)))
-            both = jnp.concatenate([high, low], axis=0).astype(BF16)
-            sums[at, :, :BLK] = both
-            sums[at, :, BLK:] = both
+        slots = range(OWNER_UNROLL * share)
+        base = n * OWNER_UNROLL * share
+        blank = jnp.zeros((2, BLK), F32)
+        lines = []
+        for u in slots:
+            line = received[n * OWNER_UNROLL + u // share, u % share * 6 : u % share * 6 + 6, :]
+            lines.append(jnp.concatenate([line, blank], axis=0))
+        spots = [jnp.where(row < 3, line, 0.0) for line in lines]
+        owns = [-0.5 * jnp.sum(spot * spot, axis=0, keepdims=True) for spot in spots]
+        left = [left_rows(jnp.where(row == 3, own, spot + fourth)) for spot, own in zip(spots, owns)]
+        right = [right_rows(jnp.where(row == 4, own, spot + third)) for spot, own in zip(spots, owns)]
+        both = []
+        for line in lines:
+            high, low = split2(jnp.where(row == 6, 1.0, jnp.where(row < 3, 0.0, line)))
+            both.append(jnp.concatenate([high.astype(F32), low.astype(F32)], axis=0).astype(BF16))
+        for u in slots:
+            at = base + u
+            lefts[at] = left[u]
+            rights[at] = right[u]
+            sums[at, :, :BLK] = both[u]
+            sums[at, :, BLK:] = both[u]
             total[at] = jnp.zeros((8, BLK), F32)
         return carry
 
@@ -392,34 +407,43 @@
 
     lax.fori_loop(0, (live + PAIR_UNROLL - 1) // PAIR_UNROLL, step, 0)
 
-    def finish(s, carry):
-        for cc in range(share):
-            found = total[s * share + cc]
-            speeds = received[s, cc * 6 + 3 : cc * 6 + 6, :]
-            out[s, cc * 3 : cc * 3 + 3, :] = speeds * found[6:7] - found[3:6]
-        return carry
-
-    lax.fori_loop(0, owners, finish, 0)
+    def finish(n, carry):
+        results = []
+        for u in range(ROW_UNROLL):
+            s = n * ROW_UNROLL + u
+            for cc in range(share):
+                found = total[s * share + cc]
+                speeds = received[s, cc * 6 + 3 : cc * 6 + 6, :]
+                results.append((s, cc, speeds * found[6:7] - found[3:6]))
+        for s, cc, force in results:
+            for c in range(3):
+                out[s, c, cc : cc + 1, :] = force[c : c + 1]
+        return carry
+
+    lax.fori_loop(0, owners // ROW_UNROLL, finish, 0)
 
 
 def finish_kernel(cut, order, returned, place_a, bond_a, place_b, bond_b, velocity, force, speed, held):
     _, grains, count = velocity.shape
     owners = returned.shape[0]
     node_blocks = count // BLK
-    share = returned.shape[1] // 3
+    share = returned.shape[2]
     blocks = held.shape[0] // (3 * grains)
 
-    def accept(d, carry):
-        for cc in range(share):
-            j = order[0, d * share + cc]
-            row = (j % blocks) * grains + j // blocks
-            for c in range(3):
-                held[pl.ds(row + c * blocks * grains, 1), :] = returned[
-                    d, cc * 3 + c : cc * 3 + c + 1, :
-                ]
-        return carry
-
-    lax.fori_loop(0, owners, accept, 0)
+    def accept(n, carry):
+        moved = []
+        for u in range(ROW_UNROLL):
+            d = n * ROW_UNROLL + u
+            for cc in range(share):
+                j = order[0, d * share + cc]
+                row = (j % blocks) * grains + j // blocks
+                for c in range(3):
+                    moved.append((row + c * blocks * grains, returned[d, c, cc : cc + 1, :]))
+        for at, line in moved:
+            held[pl.ds(at, 1), :] = line
+        return carry
+
+    lax.fori_loop(0, owners // ROW_UNROLL, accept, 0)
 
     def rows_of(early, late, group, part):
         start, end = group * 8, group * 8 + 8
@@ -433,19 +457,25 @@
 
     for group in range(grains // 8):
         rows = slice(group * 8, group * 8 + 8)
-        for tile in range(count // BLK):
+        codes = [rows_of(place_a, place_b, group, tile) for tile in range(node_blocks)]
+        low = [(code - 1) & (BLK - 1) for code in codes]
+        high = [jnp.where(code == 0, -1, (code - 1) >> 7) for code in codes]
+        found = [[jnp.zeros((8, BLK), F32)] * 3 for _ in codes]
+        for k in range(blocks):
+            sources = [
+                held[(c * blocks + k) * grains + group * 8 : (c * blocks + k) * grains + group * 8 + 8, :]
+                for c in range(3)
+            ]
+            for tile in range(node_blocks):
+                here = high[tile] == k
+                found[tile] = [
+                    jnp.where(here, jnp.take_along_axis(sources[c], low[tile], axis=1), found[tile][c])
+                    for c in range(3)
+                ]
+        for tile in range(node_blocks):
             span = slice(tile * BLK, tile * BLK + BLK)
-            code = rows_of(place_a, place_b, group, tile)
-            spot = code - 1
-            low = spot & (BLK - 1)
-            high = jnp.where(code == 0, -1, spot >> 7)
             for c in range(3):
-                total = jnp.zeros((8, BLK), F32)
-                for k in range(blocks):
-                    at = (c * blocks + k) * grains + group * 8
-                    found = jnp.take_along_axis(held[at : at + 8, :], low, axis=1)
-                    total = jnp.where(high == k, found, total)
-                total = rows_of(bond_a, bond_b, group, c * node_blocks + tile) + total
+                total = rows_of(bond_a, bond_b, group, c * node_blocks + tile) + found[tile][c]
                 force[c, rows, span] = total
                 speed[c, rows, span] = velocity[c, rows, span] + TIME_STEP * total
 
@@ -524,7 +554,7 @@
 
     slot_force = pl.pallas_call(
         contact_kernel,
-        out_shape=jax.ShapeDtypeStruct((owners, 3 * share, BLK), F32),
+        out_shape=jax.ShapeDtypeStruct((owners, 3, share, BLK), F32),
         in_specs=[smem, smem, vmem],
         out_specs=vmem,
         scratch_shapes=[

time: 50.5 us -> 48.6 us (0.962); the launches traced: 49.6 us -> 48.6 us
  starting transfers between devices: 10.5 us -> 15.8 us
  Pallas kernels: 27.2 us -> 22.3 us
  waiting for transfers between devices: 9.79 us -> 8.51 us
    pallas_call x1, Pallas kernels: 8.55 us -> 2.93 us  [on_device(): pl.pallas_call(contact_kernel, out_shape=jax.ShapeDtypeStruct((owners, 3,...]
    all_to_all x1, starting transfers between devices: 3.4 us -> 8.67 us  [on_device(): lax.all_to_all(slot_force, ('grain', 'cell'), split_axis=0, concat_axis=0...]
    all_to_all x1, waiting for transfers between devices: 5.7 us -> 4.6 us  [on_device(): lax.all_to_all(slot_force, ('grain', 'cell'), split_axis=0, concat_axis=0...]
  transfers between devices with their start and end apart: 2 -> 2, of which waited for: 2 -> 2; matrix products, arithmetic and copies ran while one was open for 0% -> 0% of each run, Pallas kernels for 23% -> 24%
where the time goes in v3:
time: 48.6 us
  Pallas kernels  22.3 us (46%)
  starting transfers between devices  15.8 us (33%)
  waiting for transfers between devices  8.51 us (18%)
  between operations  1.42 us (3%)
  local copies, waits for them, and re-layouts  0.67 us (1%)
    pallas_call x2, Pallas kernels, bonds(): pl.pallas_call(functools.partial(bond_kernel, first, part), out_shape=(ja...  11.9 us
    all_to_all x1, starting transfers between devices, on_device(): lax.all_to_all(slot_force, ('grain', 'cell'), split_axis=0, concat_axis=0...  8.67 us
    all_to_all x1, starting transfers between devices, on_device(): lax.all_to_all(outgoing, ('grain', 'cell'), split_axis=0, concat_axis=0,...  7.1 us
    all_to_all x1, waiting for transfers between devices, on_device(): lax.all_to_all(slot_force, ('grain', 'cell'), split_axis=0, concat_axis=0...  4.6 us
    pallas_call x1, Pallas kernels, on_device(): pl.pallas_call(pick_kernel, out_shape=jax.ShapeDtypeStruct((owners, 6 * s...  4.52 us
    all_to_all x1, waiting for transfers between devices, on_device(): lax.all_to_all(outgoing, ('grain', 'cell'), split_axis=0, concat_axis=0,...  3.91 us
    pallas_call x1, Pallas kernels, on_device(): pl.pallas_call(functools.partial(finish_kernel, cut), out_shape=(jax.Shap...  2.94 us
    pallas_call x1, Pallas kernels, on_device(): pl.pallas_call(contact_kernel, out_shape=jax.ShapeDtypeStruct((owners, 3,...  2.93 us
  transfers between devices with their start and end apart: 2, of which 2 were waited for; matrix products, arithmetic and copies ran while one was open for 0% of the time, Pallas kernels for 24%

profile of v3, /device:TPU:1, one launch (start us, length us, event | category | flops | bytes accessed | tf_op | source)
XLA Modules:
  0.0 48.6 jit_solution(13071037227468512799)
XLA Ops:
  0.6 0.0 copy-start.4
  0.6 4.5 %pick.1 = f32[32,24,128]{2,1,0:T(8,128)} custom-call(s32[1,128]{1,0:T(1,128)} %refs_1_.1, f32[3,32,768]{2,1,0:T(8,128)} %bitcast.12, f32[3,32,768]{2,1,0:T(8,128)} %bitcast.10, f32[3,32]{1,0:T(4,128)} %centers.1, s32[32,512]{1,0:T(8,128)} %nodes.3), custom_call_target="tpu_custom_call" | custom-call | tf_op jit(solution)/shard_map/pick/pallas_call | solution.py:501
  5.2 0.0 copy-start.1
  5.2 0.0 copy-start.2
  5.2 7.1 %all-to-all-start = ((f32[32,24,128]{2,1,0:T(8,128)}), f32[32,24,128]{2,1,0:T(8,128)S(1)}, u32[]{:S(2)}, u32[]{:S(2)}) async-start(f32[32,24,128]{2,1,0:T(8,128)} %pick.1), calls=%async_computation | async-start | bytes 786432 | tf_op jit(solution)/shard_map/all_to_all | solution.py:551
  12.3 0.0 copy-start.5
  13.0 0.0 copy-start.3
  13.0 0.0 copy-start.6
  13.0 0.0 copy-done.4
  13.0 0.0 copy-done.1
  13.0 0.0 copy-done.2
  13.0 0.0 copy-done.5
  13.0 0.6 %copy-done.3 = s32[1,128]{1,0:T(1,128)S(1)} copy-done((s32[1,128]{1,0:T(1,128)S(1)}, s32[1,128]{1,0:T(1,128)}, u32[]{:S(2)}) %copy-start.3) | copy-done | bytes 536
  13.6 0.0 copy-done.6
  13.7 7.1 %bond.2 = (f32[360,128]{1,0:T(8,128)S(1)}, s32[120,128]{1,0:T(8,128)S(1)}, s32[2,128]{1,0:T(2,128)S(1)}, s32[1,128]{1,0:T(1,128)S(1)}) custom-call(s32[8,32]{1,0:T(8,128)S(1)} %bitcast.15, f32[3,32,768]{2,1,0:T(8,128)S(1)} %bitcast.13, s32[32,4,2048]{2,1,0:T(4,128)S(1)} %copy-done.4, s32[32,512]{1,0:T(8,128)S(1)} %copy-done.2, s32[2,128]{1,0:T(2,128)S(1)} %bitcast.17, ...), custom_call_target="tpu_custom_call" | custom-call | flops 4000000000 | bytes 3000000 | tf_op jit(solution)/shard_map/bond/pallas_call | solution.py:518
  20.8 3.9 %all-to-all-done.received = f32[32,24,128]{2,1,0:T(8,128)S(1)} async-done(((f32[32,24,128]{2,1,0:T(8,128)}), f32[32,24,128]{2,1,0:T(8,128)S(1)}, u32[]{:S(2)}, u32[]{:S(2)}) %all-to-all-start) | async-done | bytes 393248 | tf_op jit(solution)/shard_map/all_to_all | solution.py:551
  24.7 2.9 %contact.1 = f32[32,3,4,128]{3,2,1,0:T(4,128)} custom-call(s32[2,128]{1,0:T(2,128)S(1)} %get-tuple-element.19.pairs, s32[1]{0:T(128)S(6)} %copy.11.count, f32[32,24,128]{2,1,0:T(8,128)S(1)} %all-to-all-done.received), custom_call_target="tpu_custom_call" | custom-call | tf_op jit(solution)/shard_map/contact/pallas_call | solution.py:555
  27.6 8.7 %all-to-all-start.1 = ((f32[32,3,4,128]{3,2,1,0:T(4,128)}), f32[32,3,4,128]{3,2,1,0:T(4,128)S(1)}, u32[]{:S(2)}, u32[]{:S(2)}) async-start(f32[32,3,4,128]{3,2,1,0:T(4,128)} %contact.1), calls=%async_computation.1 | async-start | bytes 393216 | tf_op jit(solution)/shard_map/all_to_all | solution.py:571
  36.3 0.0 copy-start
  36.3 4.7 %bond.3 = (f32[216,128]{1,0:T(8,128)S(1)}, s32[72,128]{1,0:T(8,128)S(1)}) custom-call(s32[8,32]{1,0:T(8,128)S(1)} %bitcast.16, f32[3,32,768]{2,1,0:T(8,128)S(1)} %bitcast.14, s32[32,4,2048]{2,1,0:T(4,128)S(1)} %copy-done.4, s32[32,512]{1,0:T(8,128)S(1)} %copy-done.2), custom_call_target="tpu_custom_call" | custom-call | flops 4000000000 | bytes 3000000 | tf_op jit(solution)/shard_map/bond/pallas_call | solution.py:518
  41.1 4.6 %all-to-all-done.1.returned = f32[32,3,4,128]{3,2,1,0:T(4,128)S(1)} async-done(((f32[32,3,4,128]{3,2,1,0:T(4,128)}), f32[32,3,4,128]{3,2,1,0:T(4,128)S(1)}, u32[]{:S(2)}, u32[]{:S(2)}) %all-to-all-start.1) | async-done | bytes 196640 | tf_op jit(solution)/shard_map/all_to_all | solution.py:571
  45.7 0.0 copy-done
  45.7 2.9 %finish.1 = (f32[3,32,768]{2,1,0:T(8,128)}, f32[3,32,768]{2,1,0:T(8,128)}) custom-call(s32[1,128]{1,0:T(1,128)S(1)} %get-tuple-element.18.order, f32[32,3,4,128]{3,2,1,0:T(4,128)S(1)} %all-to-all-done.1.returned, s32[120,128]{1,0:T(8,128)S(1)} %get-tuple-element.25.place_a, f32[360,128]{1,0:T(8,128)S(1)} %get-tuple-element.26.bond_a, ...), custom_call_target="tpu_custom_call" | custom-call | tf_op jit(solution)/shard_map/finish/pallas_call | solution.py:574
Async XLA Ops:
  0.6 12.4 %copy-start.4 = (s32[32,4,2048]{2,1,0:T(4,128)S(1)}, s32[32,4,2048]{2,1,0:T(4,128)}, u32[]{:S(2)}) copy-start(s32[32,4,2048]{2,1,0:T(4,128)} %bits.3) | copy-start | bytes 3145732
  5.2 7.8 %copy-start.1 = (f32[32,3,768]{2,0,1:T(8,128)S(1)}, f32[32,3,768]{2,0,1:T(8,128)}, u32[]{:S(2)}) copy-start(f32[32,3,768]{2,0,1:T(8,128)} %param.9) | copy-start | bytes 884740
  5.2 7.8 %copy-start.2 = (s32[32,512]{1,0:T(8,128)S(1)}, s32[32,512]{1,0:T(8,128)}, u32[]{:S(2)}) copy-start(s32[32,512]{1,0:T(8,128)} %nodes.3) | copy-start | bytes 196612
  5.2 19.5 %all-to-all-start = ((f32[32,24,128]{2,1,0:T(8,128)}), f32[32,24,128]{2,1,0:T(8,128)S(1)}, u32[]{:S(2)}, u32[]{:S(2)}) async-start(f32[32,24,128]{2,1,0:T(8,128)} %pick.1), calls=%async_computation | async-start | bytes 786432 | tf_op jit(solution)/shard_map/all_to_all | solution.py:551
  12.3 0.7 %copy-start.5 = (s32[32,4,2]{0,2,1:T(2,128)S(1)}, s32[32,4,2]{0,2,1:T(2,128)}, u32[]{:S(2)}) copy-start(s32[32,4,2]{0,2,1:T(2,128)} %param.12) | copy-start | bytes 3076
  13.0 0.7 %copy-start.3 = (s32[1,128]{1,0:T(1,128)S(1)}, s32[1,128]{1,0:T(1,128)}, u32[]{:S(2)}) copy-start(s32[1,128]{1,0:T(1,128)} %refs_1_.1) | copy-start | bytes 1540
  13.0 0.7 %copy-start.6 = (s32[1,128,2]{1,2,0:T(2,128)S(1)}, s32[1,128,2]{1,2,0:T(2,128)}, u32[]{:S(2)}) copy-start(s32[1,128,2]{1,2,0:T(2,128)} %param.16) | copy-start | bytes 3076
  27.6 18.1 %all-to-all-start.1 = ((f32[32,3,4,128]{3,2,1,0:T(4,128)}), f32[32,3,4,128]{3,2,1,0:T(4,128)S(1)}, u32[]{:S(2)}, u32[]{:S(2)}) async-start(f32[32,3,4,128]{3,2,1,0:T(4,128)} %contact.1), calls=%async_computation.1 | async-start | bytes 393216 | tf_op jit(solution)/shard_map/all_to_all | solution.py:571
  36.3 9.4 %copy-start = (f32[32,3,768]{2,0,1:T(8,128)S(1)}, f32[32,3,768]{2,0,1:T(8,128)}, u32[]{:S(2)}) copy-start(f32[32,3,768]{2,0,1:T(8,128)} %param.10) | copy-start | bytes 884740

commit v4 on v3

--- a/solution.py
+++ b/solution.py
@@ -22,7 +22,7 @@
 FAR_UNROLL = 4
 PAIR_UNROLL = 16
 GRAIN_UNROLL = 4
-ROW_UNROLL = 2
+ROW_UNROLL = 4
 OWNER_UNROLL = 4
 FIRST_SHARE = 5
 ALL_SHARES = 8
@@ -32,6 +32,12 @@
 
 def iota(shape, axis):
     return lax.broadcasted_iota(jnp.int32, shape, axis)
+
+
+def halves_of(number, size):
+    if size & (size - 1):
+        return lax.div(number, size), lax.rem(number, size)
+    return number >> (size.bit_length() - 1), number & (size - 1)
 
 
 def split3(value):
@@ -138,7 +144,8 @@
             d = n * ROW_UNROLL + u
             for cc in range(share):
                 j = order[0, d * share + cc]
-                row = (j % blocks) * grains + j // blocks
+                grain, k = halves_of(j, blocks)
+                row = k * grains + grain
                 for c in range(6):
                     moved.append((d, cc * 6 + c, held[pl.ds(row + c * blocks * grains, 1), :]))
         for d, at, line in moved:
@@ -252,8 +259,7 @@
             number = n * BOND_UNROLL + u
             good = number < near_count
             entry = near[jnp.where(good, number, 0)]
-            g = entry // tile_count
-            t = entry % tile_count
+            g, t = halves_of(entry, tile_count)
             a = tiles[2 * t, first + g]
             b = tiles[2 * t + 1, first + g]
             entries.append((good, g, t, g * blocks + a, g * blocks + b, b - a + 1))
@@ -302,8 +308,7 @@
             number = n * FAR_UNROLL + u
             good = number < far_count
             entry = far[jnp.where(good, number, 0)]
-            g = entry // tile_count
-            t = entry % tile_count
+            g, t = halves_of(entry, tile_count)
             a = tiles[2 * t, first + g]
             b = tiles[2 * t + 1, first + g]
             row_at = g * blocks + a
@@ -436,7 +441,8 @@
             d = n * ROW_UNROLL + u
             for cc in range(share):
                 j = order[0, d * share + cc]
-                row = (j % blocks) * grains + j // blocks
+                grain, k = halves_of(j, blocks)
+                row = k * grains + grain
                 for c in range(3):
                     moved.append((row + c * blocks * grains, returned[d, c, cc : cc + 1, :]))
         for at, line in moved:

time: 48.6 us -> 47.2 us (0.971)
  Pallas kernels: 22.3 us -> 20.9 us
    pallas_call x1, Pallas kernels: 2.94 us -> 2.36 us  [on_device(): pl.pallas_call(functools.partial(finish_kernel, cut), out_shape=(jax.Shap...]
where the time goes in v4:
time: 47.2 us; the launch traced here: 47.6 us
  Pallas kernels  20.9 us (44%)
  starting transfers between devices  16 us (34%)
  waiting for transfers between devices  8.59 us (18%)
  between operations  1.42 us (3%)
  local copies, waits for them, and re-layouts  0.67 us (1%)
    pallas_call x2, Pallas kernels, bonds(): pl.pallas_call(functools.partial(bond_kernel, first, part), out_shape=(ja...  11.6 us
    all_to_all x1, starting transfers between devices, on_device(): lax.all_to_all(slot_force, ('grain', 'cell'), split_axis=0, concat_axis=0...  8.88 us
    all_to_all x1, starting transfers between devices, on_device(): lax.all_to_all(outgoing, ('grain', 'cell'), split_axis=0, concat_axis=0,...  7.1 us
    all_to_all x1, waiting for transfers between devices, on_device(): lax.all_to_all(slot_force, ('grain', 'cell'), split_axis=0, concat_axis=0...  4.77 us
    pallas_call x1, Pallas kernels, on_device(): pl.pallas_call(pick_kernel, out_shape=jax.ShapeDtypeStruct((owners, 6 * s...  4.05 us
    all_to_all x1, waiting for transfers between devices, on_device(): lax.all_to_all(outgoing, ('grain', 'cell'), split_axis=0, concat_axis=0,...  3.82 us
    pallas_call x1, Pallas kernels, on_device(): pl.pallas_call(contact_kernel, out_shape=jax.ShapeDtypeStruct((owners, 3,...  2.88 us
    pallas_call x1, Pallas kernels, on_device(): pl.pallas_call(functools.partial(finish_kernel, cut), out_shape=(jax.Shap...  2.36 us
  transfers between devices with their start and end apart: 2, of which 2 were waited for; matrix products, arithmetic and copies ran while one was open for 0% of the time, Pallas kernels for 24%

profile of v4, /device:TPU:1, one launch (start us, length us, event | category | flops | bytes accessed | tf_op | source)
XLA Modules:
  0.0 47.6 jit_solution(18140028431915454277)
XLA Ops:
  0.6 0.0 copy-start.4
  0.6 4.1 %pick.1 = f32[32,24,128]{2,1,0:T(8,128)} custom-call(s32[1,128]{1,0:T(1,128)} %refs_1_.1, f32[3,32,768]{2,1,0:T(8,128)} %bitcast.12, f32[3,32,768]{2,1,0:T(8,128)} %bitcast.10, f32[3,32]{1,0:T(4,128)} %centers.1, s32[32,512]{1,0:T(8,128)} %nodes.3), custom_call_target="tpu_custom_call" | custom-call | tf_op jit(solution)/shard_map/pick/pallas_call | solution.py:507
  4.7 0.0 copy-start.1
  4.7 0.0 copy-start.2
  4.7 7.1 %all-to-all-start = ((f32[32,24,128]{2,1,0:T(8,128)}), f32[32,24,128]{2,1,0:T(8,128)S(1)}, u32[]{:S(2)}, u32[]{:S(2)}) async-start(f32[32,24,128]{2,1,0:T(8,128)} %pick.1), calls=%async_computation | async-start | bytes 786432 | tf_op jit(solution)/shard_map/all_to_all | solution.py:557
  11.8 0.0 copy-start.5
  12.5 0.0 copy-start.3
  12.5 0.0 copy-start.6
  12.5 0.0 copy-done.4
  12.5 0.0 copy-done.1
  12.6 0.0 copy-done.2
  12.6 0.0 copy-done.5
  12.6 0.6 %copy-done.3 = s32[1,128]{1,0:T(1,128)S(1)} copy-done((s32[1,128]{1,0:T(1,128)S(1)}, s32[1,128]{1,0:T(1,128)}, u32[]{:S(2)}) %copy-start.3) | copy-done | bytes 536
  13.2 0.0 copy-done.6
  13.2 7.2 %bond.2 = (f32[360,128]{1,0:T(8,128)S(1)}, s32[120,128]{1,0:T(8,128)S(1)}, s32[2,128]{1,0:T(2,128)S(1)}, s32[1,128]{1,0:T(1,128)S(1)}) custom-call(s32[8,32]{1,0:T(8,128)S(1)} %bitcast.15, f32[3,32,768]{2,1,0:T(8,128)S(1)} %bitcast.13, s32[32,4,2048]{2,1,0:T(4,128)S(1)} %copy-done.4, s32[32,512]{1,0:T(8,128)S(1)} %copy-done.2, s32[2,128]{1,0:T(2,128)S(1)} %bitcast.17, ...), custom_call_target="tpu_custom_call" | custom-call | flops 4000000000 | bytes 3000000 | tf_op jit(solution)/shard_map/bond/pallas_call | solution.py:524
  20.4 3.8 %all-to-all-done.received = f32[32,24,128]{2,1,0:T(8,128)S(1)} async-done(((f32[32,24,128]{2,1,0:T(8,128)}), f32[32,24,128]{2,1,0:T(8,128)S(1)}, u32[]{:S(2)}, u32[]{:S(2)}) %all-to-all-start) | async-done | bytes 393248 | tf_op jit(solution)/shard_map/all_to_all | solution.py:557
  24.2 2.9 %contact.1 = f32[32,3,4,128]{3,2,1,0:T(4,128)} custom-call(s32[2,128]{1,0:T(2,128)S(1)} %get-tuple-element.19.pairs, s32[1]{0:T(128)S(6)} %copy.11.count, f32[32,24,128]{2,1,0:T(8,128)S(1)} %all-to-all-done.received), custom_call_target="tpu_custom_call" | custom-call | tf_op jit(solution)/shard_map/contact/pallas_call | solution.py:561
  27.1 8.9 %all-to-all-start.1 = ((f32[32,3,4,128]{3,2,1,0:T(4,128)}), f32[32,3,4,128]{3,2,1,0:T(4,128)S(1)}, u32[]{:S(2)}, u32[]{:S(2)}) async-start(f32[32,3,4,128]{3,2,1,0:T(4,128)} %contact.1), calls=%async_computation.1 | async-start | bytes 393216 | tf_op jit(solution)/shard_map/all_to_all | solution.py:577
  36.0 0.0 copy-start
  36.0 4.4 %bond.3 = (f32[216,128]{1,0:T(8,128)S(1)}, s32[72,128]{1,0:T(8,128)S(1)}) custom-call(s32[8,32]{1,0:T(8,128)S(1)} %bitcast.16, f32[3,32,768]{2,1,0:T(8,128)S(1)} %bitcast.14, s32[32,4,2048]{2,1,0:T(4,128)S(1)} %copy-done.4, s32[32,512]{1,0:T(8,128)S(1)} %copy-done.2), custom_call_target="tpu_custom_call" | custom-call | flops 4000000000 | bytes 3000000 | tf_op jit(solution)/shard_map/bond/pallas_call | solution.py:524
  40.5 4.8 %all-to-all-done.1.returned = f32[32,3,4,128]{3,2,1,0:T(4,128)S(1)} async-done(((f32[32,3,4,128]{3,2,1,0:T(4,128)}), f32[32,3,4,128]{3,2,1,0:T(4,128)S(1)}, u32[]{:S(2)}, u32[]{:S(2)}) %all-to-all-start.1) | async-done | bytes 196640 | tf_op jit(solution)/shard_map/all_to_all | solution.py:577
  45.2 0.0 copy-done
  45.2 2.4 %finish.1 = (f32[3,32,768]{2,1,0:T(8,128)}, f32[3,32,768]{2,1,0:T(8,128)}) custom-call(s32[1,128]{1,0:T(1,128)S(1)} %get-tuple-element.18.order, f32[32,3,4,128]{3,2,1,0:T(4,128)S(1)} %all-to-all-done.1.returned, s32[120,128]{1,0:T(8,128)S(1)} %get-tuple-element.25.place_a, f32[360,128]{1,0:T(8,128)S(1)} %get-tuple-element.26.bond_a, ...), custom_call_target="tpu_custom_call" | custom-call | tf_op jit(solution)/shard_map/finish/pallas_call | solution.py:580
Async XLA Ops:
  0.6 11.9 %copy-start.4 = (s32[32,4,2048]{2,1,0:T(4,128)S(1)}, s32[32,4,2048]{2,1,0:T(4,128)}, u32[]{:S(2)}) copy-start(s32[32,4,2048]{2,1,0:T(4,128)} %bits.3) | copy-start | bytes 3145732
  4.7 7.8 %copy-start.1 = (f32[32,3,768]{2,0,1:T(8,128)S(1)}, f32[32,3,768]{2,0,1:T(8,128)}, u32[]{:S(2)}) copy-start(f32[32,3,768]{2,0,1:T(8,128)} %param.9) | copy-start | bytes 884740
  4.7 7.8 %copy-start.2 = (s32[32,512]{1,0:T(8,128)S(1)}, s32[32,512]{1,0:T(8,128)}, u32[]{:S(2)}) copy-start(s32[32,512]{1,0:T(8,128)} %nodes.3) | copy-start | bytes 196612
  4.7 19.5 %all-to-all-start = ((f32[32,24,128]{2,1,0:T(8,128)}), f32[32,24,128]{2,1,0:T(8,128)S(1)}, u32[]{:S(2)}, u32[]{:S(2)}) async-start(f32[32,24,128]{2,1,0:T(8,128)} %pick.1), calls=%async_computation | async-start | bytes 786432 | tf_op jit(solution)/shard_map/all_to_all | solution.py:557
  11.8 0.7 %copy-start.5 = (s32[32,4,2]{0,2,1:T(2,128)S(1)}, s32[32,4,2]{0,2,1:T(2,128)}, u32[]{:S(2)}) copy-start(s32[32,4,2]{0,2,1:T(2,128)} %param.12) | copy-start | bytes 3076
  12.5 0.7 %copy-start.3 = (s32[1,128]{1,0:T(1,128)S(1)}, s32[1,128]{1,0:T(1,128)}, u32[]{:S(2)}) copy-start(s32[1,128]{1,0:T(1,128)} %refs_1_.1) | copy-start | bytes 1540
  12.5 0.7 %copy-start.6 = (s32[1,128,2]{1,2,0:T(2,128)S(1)}, s32[1,128,2]{1,2,0:T(2,128)}, u32[]{:S(2)}) copy-start(s32[1,128,2]{1,2,0:T(2,128)} %param.16) | copy-start | bytes 3076
  27.1 18.1 %all-to-all-start.1 = ((f32[32,3,4,128]{3,2,1,0:T(4,128)}), f32[32,3,4,128]{3,2,1,0:T(4,128)S(1)}, u32[]{:S(2)}, u32[]{:S(2)}) async-start(f32[32,3,4,128]{3,2,1,0:T(4,128)} %contact.1), calls=%async_computation.1 | async-start | bytes 393216 | tf_op jit(solution)/shard_map/all_to_all | solution.py:577
  36.0 9.2 %copy-start = (f32[32,3,768]{2,0,1:T(8,128)S(1)}, f32[32,3,768]{2,0,1:T(8,128)}, u32[]{:S(2)}) copy-start(f32[32,3,768]{2,0,1:T(8,128)} %param.10) | copy-start | bytes 884740
